TPU v7x, 128 devices: a whole 4x4x4 slice. The times are simulated.
128 devices in a mesh: dp: 2 (over core), ctx: 16 (over y, x), head: 4 (over z).
Axes of the slice: x: 4, y: 4, z: 4, core: 2. Of those that a mesh axis runs over, the one named last changes fastest.
Arguments:
- group_queries: bfloat16 [4, 1024, 7168], P('dp', 'ctx', 'head'), parts along dimension 0, may hold values from -15 to 15
- group_keys: bfloat16 [4, 1024, 7168], P('dp', 'ctx', 'head'), parts along dimension 0, may hold values from -6 to 6
- group_values: bfloat16 [4, 1024, 7168], P('dp', 'ctx', 'head'), parts along dimension 0, may hold values from -6 to 6
- cache_keys: bfloat16 [4, 16384, 7168], P('dp', 'ctx', 'head'), parts along dimension 0, may hold values from -6 to 6
- cache_values: bfloat16 [4, 16384, 7168], P('dp', 'ctx', 'head'), parts along dimension 0, may hold values from -6 to 6
- cache_lengths: int32 [4], P('dp'), parts along dimension 0, may hold values from 4096 to 16384, as said below
- mamba_x: bfloat16 [4, 1024, 7168], P('dp', 'ctx', 'head'), parts along dimension 0, may hold values from -6 to 6
- mamba_bc: bfloat16 [4, 1024, 128], P('dp', 'ctx'), parts along dimension 0, may hold values from -1.5 to 1.5
- mamba_dt: bfloat16 [4, 1024, 112], P('dp', 'ctx', 'head'), parts along dimension 0, may hold values from -2.5 to 2.5
- conv_state_x: bfloat16 [4, 3, 7168], P('dp', None, 'head'), parts along dimension 0, may hold values from -6 to 6
- conv_state_bc: bfloat16 [4, 3, 128], P('dp'), parts along dimension 0, may hold values from -1.5 to 1.5
- conv_weight_x: float32 [4, 7168], P(None, 'head'), may hold values from -3 to 3
- conv_bias_x: float32 [7168], P('head'), may hold values from -3 to 3
- conv_weight_bc: float32 [4, 128], replicated, may hold values from -3 to 3
- conv_bias_bc: float32 [128], replicated, may hold values from -0.6 to 0.6
- dt_bias: float32 [112], P('head'), may hold values from 0 to 1
- a_log: float32 [112], P('head'), as said below
- skip_d: float32 [112], P('head'), may hold values from 0.5 to 1.5
- ssm_state: float32 [4, 112, 64, 64], P('dp', 'head'), parts along dimension 0, may hold values from -12 to 12
Outputs:
- attention_out: bfloat16 [4, 1024, 7168], P('dp', 'ctx', 'head'), parts along dimension 0
- mamba_out: bfloat16 [4, 1024, 7168], P('dp', 'ctx', 'head'), parts along dimension 0
There are 2 independent parts, one for each index of `dp`. A program takes and returns all parts, laid end to end along the dimension named above; an argument that names none is the same for every part. Nothing has to cross between parts.
Inputs may be any that keep to these rules, and one draw needn't show every extreme that they name: `cache_lengths`: each request's count of valid cache positions; some request has all 16384. `a_log`: log of each head's decay rate per unit of step size.
All inputs are finite; a program needn't handle non-finite values.
Results may differ from a plain program's by a relative error of at most 0.005.
Values may be sent and summed in bfloat16 or wider, within the bound.
No kernel may reach another device: no remote copies, remote signals or barrier semaphores. Data moves between devices by JAX's collectives and lax.ppermute only.
A program may use at most 256 MiB of HBM per device.

v0:
```python
import functools
import math

import jax
import jax.numpy as jnp
from jax import lax
from jax.experimental import pallas as pl
from jax.experimental.pallas import tpu as pltpu
from jax.sharding import PartitionSpec as P

HD = 224
PAD = 256
L_LANE = 224
M_LANE = 226
NEG_FILL = -1e30
EMPTY_TOP = -8192.0
HIGHEST = lax.Precision.HIGHEST
BF = jnp.bfloat16
F32 = jnp.float32
SIDE = 4
MIB = 1024 * 1024


def params(mib=16):
    return pltpu.CompilerParams(vmem_limit_bytes=mib * MIB)


def shifted(value, dy, dx):
    pairs = [
        (y * SIDE + x, ((y + dy) % SIDE) * SIDE + (x + dx) % SIDE)
        for y in range(SIDE)
        for x in range(SIDE)
    ]
    return lax.ppermute(value, "ctx", pairs)


def along(axis):
    if axis == "x":
        return lambda value, step: shifted(value, 0, step)
    return lambda value, step: shifted(value, step, 0)


def widened(block, extra):
    return jnp.concatenate([block, extra], axis=1)


def pad_cache(info, request, k_ref, gk_ref, v_ref, gv_ref, ko_ref, vo_ref):
    rows = k_ref.shape[1]
    group_rows = gk_ref.shape[1]
    first = lax.axis_index("ctx") * rows
    length = info[request]
    lane = lax.broadcasted_iota(jnp.int32, (rows, PAD - HD), 1)
    row = lax.broadcasted_iota(jnp.int32, (rows, PAD - HD), 0)
    cache_bias = jnp.where((lane == 0) & (first + row >= length), NEG_FILL, 0.0).astype(BF)
    group_bias = jnp.zeros((group_rows, PAD - HD), BF)
    ones = jnp.where(lane == 0, 1.0, 0.0).astype(BF)
    for h in range(ko_ref.shape[1]):
        window = slice(h * HD, (h + 1) * HD)
        ko_ref[0, h, :rows, :] = widened(k_ref[0, :, window], cache_bias)
        ko_ref[0, h, rows:, :] = widened(gk_ref[0, :, window], group_bias)
        vo_ref[0, h, :rows, :] = widened(v_ref[0, :, window], ones)
        vo_ref[0, h, rows:, :] = widened(gv_ref[0, :, window], ones[:group_rows])


def attend_kernel(requests, groups, pads, info, *refs):
    sets = len(groups)
    count = len(requests) * sets
    q_refs, refs = refs[:count], refs[count:]
    if pads:
        raw, refs = refs[:4], refs[4:]
        outs, (k_ref, v_ref) = refs[:count], refs[count:]
    else:
        (k_ref, v_ref), outs = refs[:2], refs[2:]
    turn = pl.program_id(0)
    here = k_ref.shape[1]
    span = q_refs[0].shape[0]
    rows = sets * span
    block = 64
    cached = k_ref.shape[2] - block
    scale = math.log2(math.e) / math.sqrt(HD)
    if pads:
        pad_cache(info, turn, *raw, k_ref, v_ref)
    position = lax.axis_index("ctx")

    def body(n):
        row = lax.broadcasted_iota(jnp.int32, (block, block), 0)
        col = lax.broadcasted_iota(jnp.int32, (block, block), 1) + position * block
        masks = []
        for group in groups:
            for lap in range(SIDE):
                along_y, along_x = (group, lap) if requests[n] == 0 else (lap, group)
                source = ((position // SIDE + along_y) % SIDE) * SIDE + (position % SIDE + along_x) % SIDE
                masks.append(col <= row + source * block)
        allowed = jnp.concatenate(masks, axis=0)
        lane = lax.broadcasted_iota(jnp.int32, (rows, PAD), 1)
        mine = q_refs[n * sets : (n + 1) * sets]

        def scored(i):
            queries = [ref[:, i * PAD : (i + 1) * PAD] for ref in mine]
            return lax.dot_general(
                jnp.concatenate(queries, axis=0) if sets > 1 else queries[0],
                k_ref[0, i],
                (((1,), (1,)), ((), ())),
                preferred_element_type=F32,
            )

        def store(i, scores):
            tail = jnp.where(allowed, scores[:, cached:], NEG_FILL)
            scores = jnp.concatenate([scores[:, :cached], tail], axis=1)
            top = jnp.maximum(jnp.max(scores, axis=1, keepdims=True) * scale, EMPTY_TOP)
            top = jnp.round(top).astype(BF).astype(F32)
            weights = jnp.exp2(scores * scale - top).astype(BF)
            out = jnp.dot(weights, v_ref[0, i], preferred_element_type=F32)
            out = jnp.where(lane == M_LANE, top, out).astype(BF)
            for at in range(sets):
                outs[n * sets + at][:, i * PAD : (i + 1) * PAD] = out[at * span : (at + 1) * span]

        scores = scored(0)
        for i in range(here):
            following = scored(i + 1) if i + 1 < here else None
            store(i, scores)
            scores = following

    for n in range(len(requests)):
        if len(requests) == 1:
            body(n)
        else:
            pl.when(turn == n)(functools.partial(body, n))


def attend(info, requests, groups, queries, keys, values, raw=None):
    sets = len(groups)
    span, width = queries[0].shape
    rows = sets * span
    heads = width // PAD
    steps = 2
    here = heads // steps
    if raw is None:
        _, _, total, _ = keys.shape
    else:
        _, cached, _ = raw[0].shape
        group_rows = raw[1].shape[1]
        total = cached + group_rows
    base = requests[0]

    def column(n):
        def at(r, g, s):
            return 0, jnp.where(r == n, g, jnp.where(r < n, 0, steps - 1))

        return at

    kv = pl.BlockSpec((1, here, total, PAD), lambda r, g, s: (base + r, g, 0, 0))
    order = [n for n in range(len(requests)) for _ in range(sets)]
    ins = [pl.BlockSpec((span, here * PAD), column(n)) for n in order]
    outs = [pl.BlockSpec((span, here * PAD), column(n)) for n in order]
    shapes = [jax.ShapeDtypeStruct((span, heads * PAD), BF)] * len(order)
    moved = 9_000_000 * len(requests) + 6 * len(requests) * rows * width
    if raw is None:
        operands, specs = [keys, values], [kv, kv]
    else:
        operands = list(raw)
        wide = pl.BlockSpec((1, cached, here * HD), lambda r, g, s: (r, 0, g))
        small = pl.BlockSpec((1, group_rows, here * HD), lambda r, g, s: (r, 0, g))
        specs = [wide, small, wide, small]
        outs += [kv, kv]
        shapes += [jax.ShapeDtypeStruct((len(requests), heads, total, PAD), BF)] * 2
        moved += 16_000_000
    work = len(requests) * heads * rows * total
    return pl.pallas_call(
        functools.partial(attend_kernel, requests, groups, raw is not None),
        grid_spec=pltpu.PrefetchScalarGridSpec(
            num_scalar_prefetch=1,
            grid=(len(requests), steps),
            in_specs=[*ins, *specs],
            out_specs=outs,
        ),
        out_shape=shapes,
        compiler_params=params(44 if raw is None and sets == 1 else 56),
        cost_estimate=pl.CostEstimate(flops=6 * work * PAD, bytes_accessed=moved, transcendentals=work),
        name="attend",
    )(info, *queries, *operands)


def join_kernel(own_ref, *refs):
    outs = refs[6:]
    rows = own_ref.shape[1]
    lane = lax.broadcasted_iota(jnp.int32, (rows, PAD - HD), 1)
    ones = jnp.where(lane == 0, 1.0, 0.0).astype(BF)
    for r, out in enumerate(outs):
        blocks = [own_ref.at[r], *refs[3 * r : 3 * r + 3]]
        for n, ref in enumerate(blocks):
            for h in range(own_ref.shape[2] // HD):
                out[n * rows : (n + 1) * rows, h * PAD : (h + 1) * PAD] = widened(
                    ref[:, h * HD : (h + 1) * HD], ones
                )


def joined_rows(own, others0, others1):
    _, rows, width = own.shape
    padded = width // HD * PAD
    return pl.pallas_call(
        join_kernel,
        out_shape=[jax.ShapeDtypeStruct((SIDE * rows, padded), BF)] * 2,
        compiler_params=params(),
        cost_estimate=pl.CostEstimate(flops=0, bytes_accessed=16 * rows * width * 2, transcendentals=0),
        name="join",
    )(own, *others0, *others1)


def merged(parts):
    tops = [part[:, M_LANE : M_LANE + 1] for part in parts]
    top = functools.reduce(jnp.maximum, tops)
    return sum(part * jnp.exp2(own - top) for part, own in zip(parts, tops)), top


def merge_kernel(*refs):
    parts, outs = refs[:4], refs[4:]
    rows = outs[0].shape[0]
    lane = lax.broadcasted_iota(jnp.int32, (rows, PAD), 1)
    for h in range(outs[0].shape[1] // PAD):
        window = slice(h * PAD, (h + 1) * PAD)
        for b in range(SIDE):
            at = slice(b * rows, (b + 1) * rows)
            total, top = merged([ref[at, window].astype(F32) for ref in parts])
            outs[b][:, window] = jnp.where(lane == M_LANE, top, total).astype(BF)


def merge(parts):
    rows, width = parts[0].shape
    steps = 2
    spec = pl.BlockSpec((rows, width // steps), lambda i: (0, i))
    out = pl.BlockSpec((rows // SIDE, width // steps), lambda i: (0, i))
    return pl.pallas_call(
        merge_kernel,
        grid=(steps,),
        in_specs=[spec] * 4,
        out_specs=[out] * 4,
        out_shape=[jax.ShapeDtypeStruct((rows // SIDE, width), BF)] * 4,
        compiler_params=params(56),
        cost_estimate=pl.CostEstimate(
            flops=rows * width * 8, bytes_accessed=rows * width * 10, transcendentals=0
        ),
        name="merge",
    )(*parts)


def finish_kernel(count, *refs):
    out_ref = refs[2 * count]
    heads = out_ref.shape[2] // HD
    for r in range(2):
        done = []
        for h in range(heads):
            window = slice(h * PAD, (h + 1) * PAD)
            total, _ = merged([ref[:, window].astype(F32) for ref in refs[r * count : (r + 1) * count]])
            done.append((total / total[:, L_LANE : L_LANE + 1])[:, :HD])
        out_ref[r] = jnp.concatenate(done, axis=1).astype(BF)


def finish(parts0, parts1):
    rows, width = parts0[0].shape
    heads = width // PAD
    return pl.pallas_call(
        functools.partial(finish_kernel, len(parts0)),
        out_shape=jax.ShapeDtypeStruct((2, rows, heads * HD), BF),
        compiler_params=params(),
        cost_estimate=pl.CostEstimate(
            flops=rows * width * 16, bytes_accessed=rows * width * 20, transcendentals=0
        ),
        name="finish",
    )(*parts0, *parts1)


def pack_kernel(x_ref, dt_ref, bc_ref, out_ref):
    rows = x_ref.shape[1]
    heads = dt_ref.shape[2]
    for r in range(2):
        extra = jnp.concatenate([dt_ref[r], jnp.zeros((rows, PAD - HD - heads), BF)], axis=1)
        for c in range(8):
            out_ref[r * 8 + c, :, :PAD] = jnp.concatenate(
                [x_ref[r, :, c * HD : (c + 1) * HD], extra], axis=1
            )
            out_ref[r * 8 + c, :, PAD:] = bc_ref[r]


def unpack_kernel(in_ref, out_ref):
    for r in range(2):
        out_ref[r] = jnp.concatenate(
            [in_ref[r * 8 + c].astype(F32)[:, :HD] for c in range(8)], axis=1
        ).astype(BF)


def split(value):
    high = value.astype(BF)
    return high, (value - high.astype(F32)).astype(BF)


def split_three(value):
    high = value.astype(BF)
    rest = value - high.astype(F32)
    middle, low = split(rest)
    return high, middle, low


def scan_kernel(
    info, data_ref, cx_ref, wx_ref, bx_ref, cb_ref, wb_ref, bb_ref, head_ref, state_ref, out_ref,
    xs_ref, bcs_ref, par_ref,
):
    tokens = data_ref.shape[0]
    chunk = 128
    request, start = info[0], info[1]
    first_head = (7 * start) // 2
    taps = wx_ref.shape[0]
    rim = taps - 1
    before = 8 - rim
    for c in range(8):

        @pl.when(start == c)
        def _():
            window = slice(c * HD, (c + 1) * HD)
            par_ref[0:taps, :HD] = wx_ref[:, window]
            par_ref[taps : taps + 1, :HD] = bx_ref[:, window]
            xs_ref[before:8, :HD] = cx_ref[request].astype(F32)[:, window]

    par_ref[:, HD:] = jnp.zeros((8, PAD - HD), F32)
    xs_ref[0:8, HD:] = jnp.zeros((8, PAD - HD), F32)
    bcs_ref[before:8, :] = cb_ref[request].astype(F32)
    xs_ref[8:, :] = data_ref[:, :PAD].astype(F32)
    bcs_ref[8:, :] = data_ref[:, PAD:].astype(F32)

    lane = lax.broadcasted_iota(jnp.int32, (8, PAD), 1) + start * HD
    head = lax.broadcasted_iota(jnp.int32, (8, PAD), 0) + first_head
    spread = (lane // 64 == head).astype(F32)
    spread3 = jnp.concatenate([spread] * 3, axis=0).astype(BF)
    pick = (
        lax.broadcasted_iota(jnp.int32, (128, 8), 0)
        == lax.broadcasted_iota(jnp.int32, (128, 8), 1) + (HD - 128) + first_head
    ).astype(F32)
    headpar = jnp.dot(head_ref[...], pick, precision=HIGHEST, preferred_element_type=F32)
    dt_bias, rate, skip = headpar[0:1], jnp.exp(headpar[1:2]), headpar[2:3]
    skip_wide = jnp.dot(skip, spread, precision=HIGHEST, preferred_element_type=F32)
    row = lax.broadcasted_iota(jnp.int32, (chunk, chunk), 0)
    col = lax.broadcasted_iota(jnp.int32, (chunk, chunk), 1)
    lower = row >= col
    lower_b = lower.astype(F32).astype(BF)
    pick_b = pick.astype(BF)
    masks = [spread[h : h + 1] for h in range(4)]
    state = jnp.concatenate(
        [state_ref[0, pl.ds(pl.multiple_of(start * HD, 32), HD), :], jnp.zeros((PAD - HD, 64), F32)], axis=0
    ).T
    for c in range(tokens // chunk):
        at = c * chunk
        x = jnp.zeros((chunk, PAD), F32) + par_ref[taps : taps + 1, :]
        bc = jnp.zeros((chunk, 128), F32) + bb_ref[...]
        for i in range(taps):
            x = x + par_ref[i : i + 1, :] * xs_ref[at + before + i : at + before + i + chunk, :]
            bc = bc + wb_ref[i : i + 1, :] * bcs_ref[at + before + i : at + before + i + chunk, :]
        x = x * jax.nn.sigmoid(x)
        bc = bc * jax.nn.sigmoid(bc)
        b, o = bc[:, :64], bc[:, 64:]
        raw = data_ref[at : at + chunk, 128:PAD]
        size = jnp.dot(raw, pick_b, preferred_element_type=F32) + dt_bias
        size = jnp.maximum(size, 0.0) + jnp.log1p(jnp.exp(-jnp.abs(size)))
        run = jnp.dot(
            lower_b, jnp.concatenate(split_three(-rate * size), axis=1), preferred_element_type=F32
        )
        run = run[:, :8] + run[:, 8:16] + run[:, 16:24]
        run_t = run.T
        wide = jnp.dot(
            jnp.concatenate(split_three(jnp.concatenate([size, run], axis=0)), axis=1),
            spread3,
            preferred_element_type=F32,
        )
        size_wide, run_wide = wide[:chunk], wide[chunk:]
        xdt = x * size_wide
        o_high, o_low = split(o)
        b_high, b_low = split(b)
        o_three = jnp.concatenate([o_high, o_high, o_low], axis=1)
        cross = lax.dot_general(
            o_three,
            jnp.concatenate([b_high, b_low, b_high], axis=1),
            (((1,), (1,)), ((), ())),
            preferred_element_type=F32,
        )
        pieces, mixes = [], []
        for h in range(4):
            gap = run[:, h : h + 1] - run_t[h : h + 1, :]
            mixes.append((jnp.exp(jnp.where(lower, gap, NEG_FILL)) * cross).astype(BF))
            pieces.append((xdt * masks[h]).astype(BF))
        y = jnp.dot(
            jnp.concatenate(mixes, axis=1), jnp.concatenate(pieces, axis=0), preferred_element_type=F32
        )
        s_high, s_low = split(state)
        y = y + jnp.exp(run_wide) * jnp.dot(
            o_three, jnp.concatenate([s_high, s_low, s_high], axis=0), preferred_element_type=F32
        )
        last = run_wide[chunk - 1 : chunk]
        w_high, w_low = split(xdt * jnp.exp(last - run_wide))
        state = state * jnp.exp(last) + lax.dot_general(
            jnp.concatenate([b_high, b_high, b_low], axis=0),
            jnp.concatenate([w_high, w_low, w_high], axis=0),
            (((0,), (0,)), ((), ())),
            preferred_element_type=F32,
        )
        out_ref[at : at + chunk, :] = (y + skip_wide * x).astype(BF)


def channels_in(mamba_x, mamba_bc, mamba_dt):
    rows = mamba_x.shape[1]
    packed = pl.pallas_call(
        pack_kernel,
        out_shape=jax.ShapeDtypeStruct((16, rows, PAD + 128), BF),
        compiler_params=params(),
        name="pack",
    )(mamba_x, mamba_dt, mamba_bc)
    return packed, lax.all_to_all(packed, "ctx", 0, 0, tiled=True).reshape(16 * rows, PAD + 128)


def state_space(
    position, mine, conv_state_x, conv_state_bc, conv_weight_x, conv_bias_x, conv_weight_bc,
    conv_bias_bc, dt_bias, a_log, skip_d, ssm_state,
):
    rows = mine.shape[0] // 16
    heads = dt_bias.shape[0]
    headpar = jnp.pad(jnp.stack([dt_bias, a_log, skip_d]), ((0, 5), (HD - 128, 128 - (HD - 128) - heads)))
    state = ssm_state.reshape(2, -1, 64)
    tokens = 16 * rows

    def whole(value):
        return pl.BlockSpec(value.shape, lambda i, s: (0,) * value.ndim)

    operands = (
        mine, conv_state_x, conv_weight_x, conv_bias_x[None], conv_state_bc, conv_weight_bc,
        conv_bias_bc[None], headpar,
    )
    out = pl.pallas_call(
        scan_kernel,
        grid_spec=pltpu.PrefetchScalarGridSpec(
            num_scalar_prefetch=1,
            grid=(1,),
            in_specs=[*map(whole, operands), pl.BlockSpec((1, *state.shape[1:]), lambda i, s: (s[0], 0, 0))],
            out_specs=pl.BlockSpec((tokens, PAD), lambda i, s: (0, 0)),
            scratch_shapes=[
                pltpu.VMEM((tokens + 8, PAD), F32),
                pltpu.VMEM((tokens + 8, 128), F32),
                pltpu.VMEM((8, PAD), F32),
            ],
        ),
        out_shape=jax.ShapeDtypeStruct((tokens, PAD), BF),
        compiler_params=params(28),
        cost_estimate=pl.CostEstimate(
            flops=8_000_000_000, bytes_accessed=2_500_000, transcendentals=2_000_000
        ),
        name="scan",
    )(jnp.stack([position // 8, position % 8]).astype(jnp.int32), *operands, state)
    return out.reshape(16, rows, PAD)


def unpacked(back):
    return pl.pallas_call(
        unpack_kernel,
        out_shape=jax.ShapeDtypeStruct((2, back.shape[1], 8 * HD), BF),
        compiler_params=params(),
        name="unpack",
    )(back)


def after(values, done):
    return lax.optimization_barrier((values, done))[0]


def sent_home(one, two, three, axis):
    move = along(axis)
    return [move(one, 1), move(three, -1), move(two, 2)]


def per_device(
    group_queries, group_keys, group_values, cache_keys, cache_values, cache_lengths, mamba_x, mamba_bc,
    mamba_dt, conv_state_x, conv_state_bc, conv_weight_x, conv_bias_x, conv_weight_bc, conv_bias_bc,
    dt_bias, a_log, skip_d, ssm_state,
):
    position = lax.axis_index("ctx")
    info = cache_lengths
    queries = [group_queries[0], group_queries[1]]
    moves = [along("x"), along("y")]
    others = [[move(q, -1), move(q, 2), move(q, 1)] for q, move in zip(queries, moves)]
    packed, mine = channels_in(after(mamba_x, others[0][0]), mamba_bc, mamba_dt)
    first0, first1 = joined_rows(after(group_queries, packed), *others)
    far0, far1 = moves[1](first0, 2), moves[0](first1, 2)
    own0, own1, keys, values = attend(
        info, (0, 1), (0,), [first0, first1], None, None,
        (cache_keys, group_keys, cache_values, group_values),
    )
    first0, first1 = after((first0, first1), (far0, far1, own0))
    after0, before0 = moves[1](first0, -1), moves[1](first0, 1)
    after1, before1 = moves[0](first1, -1), moves[0](first1, 1)
    two0, two1 = attend(after(info, own0), (0, 1), (2,), [far0, far1], keys, values)
    scan_inputs = (
        mine, conv_state_x, conv_state_bc, conv_weight_x, conv_bias_x, conv_weight_bc, conv_bias_bc,
        dt_bias, a_log, skip_d, ssm_state,
    )
    scanned = state_space(position, *after(scan_inputs, two0))
    two0, two1 = after((two0, two1), (after0, before0, after1, before1))
    one0, three0, one1, three1 = attend(
        after(info, (two0, scanned)), (0, 1), (1, 3), [after0, before0, after1, before1], keys, values
    )
    back = lax.all_to_all(after(scanned, one0), "ctx", 0, 0, tiled=True)
    two0, two1 = moves[1](two0, 2), moves[0](two1, 2)
    side0 = [moves[1](one0, 1), moves[1](three0, -1)]
    three1 = after(three1, (two0, two1))
    side1 = [moves[0](one1, 1), moves[0](three1, -1)]
    blocks0 = merge([after(own0, scanned), *side0, two0])
    home0 = [blocks0[0], *sent_home(*blocks0[1:], "x")]
    blocks1 = merge([after(own1, blocks0[0]), *side1, two1])
    blocks1 = after(blocks1, back)
    home1 = [blocks1[0], *sent_home(*blocks1[1:], "y")]
    return finish(home0, home1), unpacked(back)


def solution(mesh):
    token = P("dp", "ctx", "head")
    placed = (
        token, token, token, token, token, P("dp"), token, P("dp", "ctx", None), token,
        P("dp", None, "head"), P("dp", None, None), P(None, "head"), P("head"), P(), P(),
        P("head"), P("head"), P("head"), P("dp", "head", None, None),
    )
    return jax.shard_map(
        per_device, mesh=mesh, in_specs=placed, out_specs=(token, token), check_vma=False
    )
```

profile of v0, /device:TPU:0, one launch (start us, length us, event | category | flops | bytes accessed | tf_op | source)
XLA Modules:
  0.0 160.3 jit_solution(8463387061822755424)
XLA Ops:
  0.6 1.1 slice_bitcast_fusion
  1.7 2.9 %collective-permute-start = (bf16[64,1792]{1,0:T(8,128)(2,1)S(1)}, bf16[64,1792]{1,0:T(8,128)(2,1)S(1)}, u32[]{:S(2)}, u32[]{:S(2)}) collective-permute-start(bf16[64,1792]{1,0:T(8,128)(2,1)S(1)} %get-tuple-element.97), channel_id=1, source_target_pairs={{0,12},{4,0},{8,4},{12,8},{16,28},{20,16},{24,20},{28,24},{32,44},... | collective-permute-start | bytes 688136 | tf_op jit(solution)/shard_map/ppermute | solution.py:34
  4.6 1.6 collective-permute-start.5
  6.2 2.9 %collective-permute-start.4 = (bf16[64,1792]{1,0:T(8,128)(2,1)S(1)}, bf16[64,1792]{1,0:T(8,128)(2,1)S(1)}, u32[]{:S(2)}, u32[]{:S(2)}) collective-permute-start(bf16[64,1792]{1,0:T(8,128)(2,1)S(1)} %get-tuple-element.96), channel_id=1, source_target_pairs={{0,32},{4,36},{8,40},{12,44},{16,48},{20,52},{24,56},{28,60},{32,0... | collective-permute-start | bytes 688136 | tf_op jit(solution)/shard_map/ppermute | solution.py:34
  9.1 1.3 collective-permute-start.3
  10.5 2.3 %collective-permute-start.1 = (bf16[64,1792]{1,0:T(8,128)(2,1)S(1)}, bf16[64,1792]{1,0:T(8,128)(2,1)S(1)}, u32[]{:S(2)}, u32[]{:S(2)}) collective-permute-start(bf16[64,1792]{1,0:T(8,128)(2,1)S(1)} %get-tuple-element.97), channel_id=1, source_target_pairs={{0,8},{4,12},{8,0},{12,4},{16,24},{20,28},{24,16},{28,20},{32,40},... | collective-permute-start | bytes 688136 | tf_op jit(solution)/shard_map/ppermute | solution.py:34
  12.7 0.8 copy.21.dt_ref
  13.6 1.0 copy-done.1
  14.6 0.8 copy-done.4
  15.4 1.1 pack.1
  16.5 2.6 %collective-permute-done.4.refs_4_ = bf16[64,1792]{1,0:T(8,128)(2,1)S(1)} collective-permute-done((bf16[64,1792]{1,0:T(8,128)(2,1)S(1)}, bf16[64,1792]{1,0:T(8,128)(2,1)S(1)}, u32[]{:S(2)}, u32[]{:S(2)}) %collective-permute-start.4) | collective-permute-done | bytes 229408 | tf_op jit(solution)/shard_map/ppermute | solution.py:34
  19.1 3.7 %collective-permute-done.2.refs_2_ = bf16[64,1792]{1,0:T(8,128)(2,1)S(1)} collective-permute-done((bf16[64,1792]{1,0:T(8,128)(2,1)S(1)}, bf16[64,1792]{1,0:T(8,128)(2,1)S(1)}, u32[]{:S(2)}, u32[]{:S(2)}) %collective-permute-start.2) | collective-permute-done | bytes 229408 | tf_op jit(solution)/shard_map/ppermute | solution.py:34
  22.8 1.0 copy-done
  23.8 0.7 join.1
  24.5 0.5 collective-permute-start.6
  25.0 0.6 collective-permute-start.7
  25.6 0.1 pad_add_fusion.info
  25.6 6.9 %all-to-all-start = ((bf16[16,64,384]{2,1,0:T(8,128)(2,1)}), bf16[16,64,384]{2,1,0:T(8,128)(2,1)S(1)}, u32[]{:S(2)}, u32[]{:S(2)}) async-start(bf16[16,64,384]{2,1,0:T(8,128)(2,1)} %pack.1), calls=%async_computation | async-start | bytes 1572864 | tf_op jit(solution)/shard_map/all_to_all | solution.py:415
  32.6 0.0 copy-start.15
  32.6 19.3 %attend.3 = (bf16[256,2048]{1,0:T(8,128)(2,1)}, bf16[256,2048]{1,0:T(8,128)(2,1)}, bf16[2,8,1088,256]{3,2,1,0:T(8,128)(2,1)}, bf16[2,8,1088,256]{3,2,1,0:T(8,128)(2,1)}) custom-call(s32[2]{0:T(128)} %info.3, bf16[256,2048]{1,0:T(8,128)(2,1)} %copy-done.7, bf16[256,2048]{1,0:T(8,128)(2,1)} %copy-done.6, bf16[2,1024,1792]{2,1,0:T(8,128)(2,1)} %refs_2_.1, ...), custom_call_target="tpu_custom_call" | custom-call | flops 6845104128 | bytes 40291456 | tf_op jit(solution)/shard_map/attend/pallas_call | solution.py:169
  51.9 1.2 collective-permute-done.6.refs_0_
  53.1 0.8 collective-permute-start.9
  53.9 2.5 %collective-permute-start.8 = (bf16[256,2048]{1,0:T(8,128)(2,1)}, bf16[256,2048]{1,0:T(8,128)(2,1)}, u32[]{:S(2)}, u32[]{:S(2)}) collective-permute-start(bf16[256,2048]{1,0:T(8,128)(2,1)} %copy-done.7), channel_id=1, source_target_pairs={{0,48},{4,52},{8,56},{12,60},{16,0},{20,4},{24,8},{28,12},{32,16},... | collective-permute-start | bytes 3145736 | tf_op jit(solution)/shard_map/ppermute | solution.py:34
  56.4 0.8 collective-permute-start.11
  57.1 2.5 %collective-permute-start.10 = (bf16[256,2048]{1,0:T(8,128)(2,1)}, bf16[256,2048]{1,0:T(8,128)(2,1)}, u32[]{:S(2)}, u32[]{:S(2)}) collective-permute-start(bf16[256,2048]{1,0:T(8,128)(2,1)} %copy-done.6), channel_id=1, source_target_pairs={{0,12},{4,0},{8,4},{12,8},{16,28},{20,16},{24,20},{28,24},{32,44},... | collective-permute-start | bytes 3145736 | tf_op jit(solution)/shard_map/ppermute | solution.py:34
  59.6 0.0 copy-start.22
  59.6 0.0 copy-start.23
  59.6 0.0 copy-start.24
  59.6 0.0 copy-start.5
  59.7 0.0 copy-start.12
  59.7 0.0 copy-start.13
  59.7 0.0 copy-start.14
  59.7 11.5 %attend.4 = (bf16[256,2048]{1,0:T(8,128)(2,1)S(1)}, bf16[256,2048]{1,0:T(8,128)(2,1)S(1)}) custom-call(s32[2]{0:T(128)S(1)} %copy-done.15, bf16[256,2048]{1,0:T(8,128)(2,1)} %collective-permute-done.6.refs_0_, bf16[256,2048]{1,0:T(8,128)(2,1)} %collective-permute-done.7.refs_1_, bf16[2,8,1088,256]{3,2,1,0:T(8,128)(2,1)} %get-tuple-element.55.refs_2_.refs_4_, ...), custom_call_target="tpu_custom_call" | custom-call | flops 6845104128 | bytes 24291456 | tf_op jit(solution)/shard_map/attend/pallas_call | solution.py:169
  71.2 1.0 copy-done.8
  72.2 1.0 copy-done.10
  73.3 0.1 select_maximum_fusion.head_ref
  73.4 8.4 %scan.1 = bf16[1024,256]{1,0:T(8,128)(2,1)} custom-call(s32[2]{0:T(128)S(1)} %pad_add_fusion.info, bf16[1024,384]{1,0:T(8,128)(2,1)S(1)} %bitcast.13, bf16[2,3,1792]{2,1,0:T(4,128)(2,1)S(1)} %copy.22.cx_ref, f32[4,1792]{1,0:T(4,128)S(1)} %copy-done.12, f32[1,1792]{1,0:T(1,128)S(1)} %broadcast_in_dim.6.bx_ref, bf16[2,3,128]{2,1,0:T(4,128)(2,1)S(1)} %copy.23.cb_ref, ...), custom_call_target="tpu_custom_call" | custom-call | flops 8000000000 | bytes 2500000 | tf_op jit(solution)/shard_map/scan/pallas_call | solution.py:435
  81.8 1.4 collective-permute-start.14
  83.2 1.6 collective-permute-start.19
  84.7 18.7 %attend.5 = (bf16[256,2048]{1,0:T(8,128)(2,1)}, bf16[256,2048]{1,0:T(8,128)(2,1)}, bf16[256,2048]{1,0:T(8,128)(2,1)}, bf16[256,2048]{1,0:T(8,128)(2,1)}) custom-call(s32[2]{0:T(128)} %info.3, bf16[256,2048]{1,0:T(8,128)(2,1)} %collective-permute-done.8.refs_0_, bf16[256,2048]{1,0:T(8,128)(2,1)} %collective-permute-done.9.refs_1_, ...), custom_call_target="tpu_custom_call" | custom-call | flops 13690208256 | bytes 30582912 | tf_op jit(solution)/shard_map/attend/pallas_call | solution.py:169
  103.5 1.2 collective-permute-start.13
  104.7 0.8 collective-permute-start.12
  105.5 0.6 collective-permute-start.18
  106.0 0.6 collective-permute-done.19.refs_3_
  106.7 1.1 copy-done.18
  107.8 2.0 %collective-permute-start.20 = (bf16[256,2048]{1,0:T(8,128)(2,1)}, bf16[256,2048]{1,0:T(8,128)(2,1)}, u32[]{:S(2)}, u32[]{:S(2)}) collective-permute-start(bf16[256,2048]{1,0:T(8,128)(2,1)} %get-tuple-element.86), channel_id=1, source_target_pairs={{0,12},{4,0},{8,4},{12,8},{16,28},{20,16},{24,20},{28,24},{32,44},... | collective-permute-start | bytes 3145736 | tf_op jit(solution)/shard_map/ppermute | solution.py:34
  109.8 4.7 %all-to-all-start.1 = ((bf16[16,64,256]{2,1,0:T(8,128)(2,1)}), bf16[16,64,256]{2,1,0:T(8,128)(2,1)S(1)}, u32[]{:S(2)}, u32[]{:S(2)}) async-start(bf16[16,64,256]{2,1,0:T(8,128)(2,1)} %bitcast.10), calls=%async_computation.1 | async-start | bytes 1048576 | tf_op jit(solution)/shard_map/all_to_all | solution.py:506
  114.6 13.4 %collective-permute-done.13.refs_2_ = bf16[256,2048]{1,0:T(8,128)(2,1)} collective-permute-done((bf16[256,2048]{1,0:T(8,128)(2,1)}, bf16[256,2048]{1,0:T(8,128)(2,1)}, u32[]{:S(2)}, u32[]{:S(2)}) %collective-permute-start.13) | collective-permute-done | bytes 1048608 | tf_op jit(solution)/shard_map/ppermute | solution.py:34
  128.0 3.5 %collective-permute-done.12.refs_1_ = bf16[256,2048]{1,0:T(8,128)(2,1)} collective-permute-done((bf16[256,2048]{1,0:T(8,128)(2,1)}, bf16[256,2048]{1,0:T(8,128)(2,1)}, u32[]{:S(2)}, u32[]{:S(2)}) %collective-permute-start.12) | collective-permute-done | bytes 1048608 | tf_op jit(solution)/shard_map/ppermute | solution.py:34
  131.4 4.0 %merge.2 = (bf16[64,2048]{1,0:T(8,128)(2,1)}, bf16[64,2048]{1,0:T(8,128)(2,1)}, bf16[64,2048]{1,0:T(8,128)(2,1)}, bf16[64,2048]{1,0:T(8,128)(2,1)}) custom-call(bf16[256,2048]{1,0:T(8,128)(2,1)} %get-tuple-element.69.refs_0_, bf16[256,2048]{1,0:T(8,128)(2,1)} %collective-permute-done.12.refs_1_, bf16[256,2048]{1,0:T(8,128)(2,1)} %collective-permute-done.13.refs_2_, ...), custom_call_target="tpu_custom_call" | custom-call | flops 4194304 | bytes 5242880 | tf_op jit(solution)/shard_map/merge/pallas_call | solution.py:233
  135.5 0.0 collective-permute-start.15
  135.5 3.2 %collective-permute-start.16 = (bf16[64,2048]{1,0:T(8,128)(2,1)}, bf16[64,2048]{1,0:T(8,128)(2,1)S(1)}, u32[]{:S(2)}, u32[]{:S(2)}) collective-permute-start(bf16[64,2048]{1,0:T(8,128)(2,1)} %get-tuple-element.79), channel_id=1, source_target_pairs={{0,12},{4,0},{8,4},{12,8},{16,28},{20,16},{24,20},{28,24},{32,44},... | collective-permute-start | bytes 786440 | tf_op jit(solution)/shard_map/ppermute | solution.py:34
  138.7 0.6 collective-permute-start.17
  139.3 1.0 copy-done.17
  140.2 4.1 %merge.3 = (bf16[64,2048]{1,0:T(8,128)(2,1)}, bf16[64,2048]{1,0:T(8,128)(2,1)}, bf16[64,2048]{1,0:T(8,128)(2,1)}, bf16[64,2048]{1,0:T(8,128)(2,1)}) custom-call(bf16[256,2048]{1,0:T(8,128)(2,1)} %get-tuple-element.82.refs_0_, bf16[256,2048]{1,0:T(8,128)(2,1)} %copy-done.17, bf16[256,2048]{1,0:T(8,128)(2,1)} %collective-permute-done.20.refs_2_, ...), custom_call_target="tpu_custom_call" | custom-call | flops 4194304 | bytes 5242880 | tf_op jit(solution)/shard_map/merge/pallas_call | solution.py:233
  144.3 0.4 collective-permute-start.21
  144.7 2.9 %collective-permute-start.22 = (bf16[64,2048]{1,0:T(8,128)(2,1)}, bf16[64,2048]{1,0:T(8,128)(2,1)S(1)}, u32[]{:S(2)}, u32[]{:S(2)}) collective-permute-start(bf16[64,2048]{1,0:T(8,128)(2,1)} %get-tuple-element.94), channel_id=1, source_target_pairs={{0,48},{4,52},{8,56},{12,60},{16,0},{20,4},{24,8},{28,12},{32,16},... | collective-permute-start | bytes 786440 | tf_op jit(solution)/shard_map/ppermute | solution.py:34
  147.6 0.9 unpack.1
  148.6 3.6 %collective-permute-done.21.refs_5_ = bf16[64,2048]{1,0:T(8,128)(2,1)S(1)} collective-permute-done((bf16[64,2048]{1,0:T(8,128)(2,1)}, bf16[64,2048]{1,0:T(8,128)(2,1)S(1)}, u32[]{:S(2)}, u32[]{:S(2)}) %collective-permute-start.21) | collective-permute-done | bytes 262176 | tf_op jit(solution)/shard_map/ppermute | solution.py:34
  152.2 2.5 %collective-permute-done.22.refs_6_ = bf16[64,2048]{1,0:T(8,128)(2,1)S(1)} collective-permute-done((bf16[64,2048]{1,0:T(8,128)(2,1)}, bf16[64,2048]{1,0:T(8,128)(2,1)S(1)}, u32[]{:S(2)}, u32[]{:S(2)}) %collective-permute-start.22) | collective-permute-done | bytes 262176 | tf_op jit(solution)/shard_map/ppermute | solution.py:34
  154.6 1.1 collective-permute-done.23.refs_7_
  155.7 0.9 copy-done.2
  156.6 0.9 copy-done.3
  157.6 2.7 %finish.1 = bf16[2,64,1792]{2,1,0:T(8,128)(2,1)} custom-call(bf16[64,2048]{1,0:T(8,128)(2,1)S(1)} %copy-done.2, bf16[64,2048]{1,0:T(8,128)(2,1)S(1)} %collective-permute-done.15.refs_1_, bf16[64,2048]{1,0:T(8,128)(2,1)S(1)} %collective-permute-done.16.refs_2_, bf16[64,2048]{1,0:T(8,128)(2,1)S(1)} %collective-permute-done.17.refs_3_, ...), custom_call_target="tpu_custom_call" | custom-call | flops 2097152 | bytes 2621440 | tf_op jit(solution)/shard_map/finish/pallas_call | solution.py:262
  (55 shorter events, 0.1 us)
Async XLA Ops:
  1.7 8.7 %collective-permute-start = (bf16[64,1792]{1,0:T(8,128)(2,1)S(1)}, bf16[64,1792]{1,0:T(8,128)(2,1)S(1)}, u32[]{:S(2)}, u32[]{:S(2)}) collective-permute-start(bf16[64,1792]{1,0:T(8,128)(2,1)S(1)} %get-tuple-element.97), channel_id=1, source_target_pairs={{0,12},{4,0},{8,4},{12,8},{16,28},{20,16},{24,20},{28,24},{32,44},... | collective-permute-start | bytes 688136 | tf_op jit(solution)/shard_map/ppermute | solution.py:34
  4.6 11.9 %collective-permute-start.5 = (bf16[64,1792]{1,0:T(8,128)(2,1)S(1)}, bf16[64,1792]{1,0:T(8,128)(2,1)S(1)}, u32[]{:S(2)}, u32[]{:S(2)}) collective-permute-start(bf16[64,1792]{1,0:T(8,128)(2,1)S(1)} %get-tuple-element.96), channel_id=1, source_target_pairs={{0,16},{4,20},{8,24},{12,28},{16,32},{20,36},{24,40},{28,44},{32,4... | collective-permute-start | bytes 688136 | tf_op jit(solution)/shard_map/ppermute | solution.py:34
  6.2 12.9 %collective-permute-start.4 = (bf16[64,1792]{1,0:T(8,128)(2,1)S(1)}, bf16[64,1792]{1,0:T(8,128)(2,1)S(1)}, u32[]{:S(2)}, u32[]{:S(2)}) collective-permute-start(bf16[64,1792]{1,0:T(8,128)(2,1)S(1)} %get-tuple-element.96), channel_id=1, source_target_pairs={{0,32},{4,36},{8,40},{12,44},{16,48},{20,52},{24,56},{28,60},{32,0... | collective-permute-start | bytes 688136 | tf_op jit(solution)/shard_map/ppermute | solution.py:34
  9.1 10.0 %collective-permute-start.3 = (bf16[64,1792]{1,0:T(8,128)(2,1)S(1)}, bf16[64,1792]{1,0:T(8,128)(2,1)S(1)}, u32[]{:S(2)}, u32[]{:S(2)}) collective-permute-start(bf16[64,1792]{1,0:T(8,128)(2,1)S(1)} %get-tuple-element.96), channel_id=1, source_target_pairs={{0,48},{4,52},{8,56},{12,60},{16,0},{20,4},{24,8},{28,12},{32,16},... | collective-permute-start | bytes 688136 | tf_op jit(solution)/shard_map/ppermute | solution.py:34
  10.5 12.3 %collective-permute-start.2 = (bf16[64,1792]{1,0:T(8,128)(2,1)S(1)}, bf16[64,1792]{1,0:T(8,128)(2,1)S(1)}, u32[]{:S(2)}, u32[]{:S(2)}) collective-permute-start(bf16[64,1792]{1,0:T(8,128)(2,1)S(1)} %get-tuple-element.97), channel_id=1, source_target_pairs={{0,4},{4,8},{8,12},{12,0},{16,20},{20,24},{24,28},{28,16},{32,36},... | collective-permute-start | bytes 688136 | tf_op jit(solution)/shard_map/ppermute | solution.py:34
  10.5 12.3 %collective-permute-start.1 = (bf16[64,1792]{1,0:T(8,128)(2,1)S(1)}, bf16[64,1792]{1,0:T(8,128)(2,1)S(1)}, u32[]{:S(2)}, u32[]{:S(2)}) collective-permute-start(bf16[64,1792]{1,0:T(8,128)(2,1)S(1)} %get-tuple-element.97), channel_id=1, source_target_pairs={{0,8},{4,12},{8,0},{12,4},{16,24},{20,28},{24,16},{28,20},{32,40},... | collective-permute-start | bytes 688136 | tf_op jit(solution)/shard_map/ppermute | solution.py:34
  13.6 1.0 copy-start.1
  14.6 0.8 copy-start.4
  22.8 1.0 copy-start
  24.5 8.1 %copy-start.6 = (bf16[256,2048]{1,0:T(8,128)(2,1)}, bf16[256,2048]{1,0:T(8,128)(2,1)S(1)}, u32[]{:S(2)}) copy-start(bf16[256,2048]{1,0:T(8,128)(2,1)S(1)} %get-tuple-element.72.refs_1_) | copy-start | bytes 3145732
  24.5 8.1 %copy-start.7 = (bf16[256,2048]{1,0:T(8,128)(2,1)}, bf16[256,2048]{1,0:T(8,128)(2,1)S(1)}, u32[]{:S(2)}) copy-start(bf16[256,2048]{1,0:T(8,128)(2,1)S(1)} %get-tuple-element.71.refs_0_) | copy-start | bytes 3145732
  24.5 28.6 %collective-permute-start.6 = (bf16[256,2048]{1,0:T(8,128)(2,1)S(1)}, bf16[256,2048]{1,0:T(8,128)(2,1)}, u32[]{:S(2)}, u32[]{:S(2)}) collective-permute-start(bf16[256,2048]{1,0:T(8,128)(2,1)S(1)} %get-tuple-element.71.refs_0_), channel_id=1, source_target_pairs={{0,32},{4,36},{8,40},{12,44},{16,48},{20,52},{24,56},{28,60},{32,0... | collective-permute-start | bytes 3145736 | tf_op jit(solution)/shard_map/ppermute | solution.py:34
  25.0 28.1 %collective-permute-start.7 = (bf16[256,2048]{1,0:T(8,128)(2,1)S(1)}, bf16[256,2048]{1,0:T(8,128)(2,1)}, u32[]{:S(2)}, u32[]{:S(2)}) collective-permute-start(bf16[256,2048]{1,0:T(8,128)(2,1)S(1)} %get-tuple-element.72.refs_1_), channel_id=1, source_target_pairs={{0,8},{4,12},{8,0},{12,4},{16,24},{20,28},{24,16},{28,20},{32,40},... | collective-permute-start | bytes 3145736 | tf_op jit(solution)/shard_map/ppermute | solution.py:34
  25.6 47.5 %all-to-all-start = ((bf16[16,64,384]{2,1,0:T(8,128)(2,1)}), bf16[16,64,384]{2,1,0:T(8,128)(2,1)S(1)}, u32[]{:S(2)}, u32[]{:S(2)}) async-start(bf16[16,64,384]{2,1,0:T(8,128)(2,1)} %pack.1), calls=%async_computation | async-start | bytes 1572864 | tf_op jit(solution)/shard_map/all_to_all | solution.py:415
  32.6 27.0 %copy-start.15 = (s32[2]{0:T(128)S(1)}, s32[2]{0:T(128)}, u32[]{:S(2)}) copy-start(s32[2]{0:T(128)} %info.3) | copy-start | bytes 28
  53.1 28.7 %collective-permute-start.9 = (bf16[256,2048]{1,0:T(8,128)(2,1)}, bf16[256,2048]{1,0:T(8,128)(2,1)}, u32[]{:S(2)}, u32[]{:S(2)}) collective-permute-start(bf16[256,2048]{1,0:T(8,128)(2,1)} %copy-done.7), channel_id=1, source_target_pairs={{0,16},{4,20},{8,24},{12,28},{16,32},{20,36},{24,40},{28,44},{32,4... | collective-permute-start | bytes 3145736 | tf_op jit(solution)/shard_map/ppermute | solution.py:34
  53.9 27.9 %collective-permute-start.8 = (bf16[256,2048]{1,0:T(8,128)(2,1)}, bf16[256,2048]{1,0:T(8,128)(2,1)}, u32[]{:S(2)}, u32[]{:S(2)}) collective-permute-start(bf16[256,2048]{1,0:T(8,128)(2,1)} %copy-done.7), channel_id=1, source_target_pairs={{0,48},{4,52},{8,56},{12,60},{16,0},{20,4},{24,8},{28,12},{32,16},... | collective-permute-start | bytes 3145736 | tf_op jit(solution)/shard_map/ppermute | solution.py:34
  56.4 25.4 %collective-permute-start.11 = (bf16[256,2048]{1,0:T(8,128)(2,1)}, bf16[256,2048]{1,0:T(8,128)(2,1)}, u32[]{:S(2)}, u32[]{:S(2)}) collective-permute-start(bf16[256,2048]{1,0:T(8,128)(2,1)} %copy-done.6), channel_id=1, source_target_pairs={{0,4},{4,8},{8,12},{12,0},{16,20},{20,24},{24,28},{28,16},{32,36},... | collective-permute-start | bytes 3145736 | tf_op jit(solution)/shard_map/ppermute | solution.py:34
  57.1 24.7 %collective-permute-start.10 = (bf16[256,2048]{1,0:T(8,128)(2,1)}, bf16[256,2048]{1,0:T(8,128)(2,1)}, u32[]{:S(2)}, u32[]{:S(2)}) collective-permute-start(bf16[256,2048]{1,0:T(8,128)(2,1)} %copy-done.6), channel_id=1, source_target_pairs={{0,12},{4,0},{8,4},{12,8},{16,28},{20,16},{24,20},{28,24},{32,44},... | collective-permute-start | bytes 3145736 | tf_op jit(solution)/shard_map/ppermute | solution.py:34
  59.6 13.6 %copy-start.21 = (bf16[2,3,128]{2,0,1:T(2,128)(2,1)S(1)}, bf16[2,3,128]{2,0,1:T(2,128)(2,1)}, u32[]{:S(2)}) copy-start(bf16[2,3,128]{2,0,1:T(2,128)(2,1)} %param.29) | copy-start | bytes 4612
  59.6 13.6 %copy-start.20 = (f32[1792]{0:T(1024)S(1)}, f32[1792]{0:T(1024)}, u32[]{:S(2)}) copy-start(f32[1792]{0:T(1024)} %param.31) | copy-start | bytes 21508
  59.6 13.6 %copy-start.19 = (bf16[2,3,1792]{2,0,1:T(2,128)(2,1)S(1)}, bf16[2,3,1792]{2,0,1:T(2,128)(2,1)}, u32[]{:S(2)}) copy-start(bf16[2,3,1792]{2,0,1:T(2,128)(2,1)} %param.28) | copy-start | bytes 64516
  59.6 13.6 %copy-start.22 = (f32[28]{0:T(128)S(1)}, f32[28]{0:T(128)}, u32[]{:S(2)}) copy-start(f32[28]{0:T(128)} %param.36) | copy-start | bytes 340
  59.6 13.6 %copy-start.23 = (f32[28]{0:T(128)S(1)}, f32[28]{0:T(128)}, u32[]{:S(2)}) copy-start(f32[28]{0:T(128)} %param.35) | copy-start | bytes 340
  59.6 13.6 %copy-start.24 = (f32[28]{0:T(128)S(1)}, f32[28]{0:T(128)}, u32[]{:S(2)}) copy-start(f32[28]{0:T(128)} %param.34) | copy-start | bytes 340
  59.6 13.7 %copy-start.5 = (f32[2,28,64,64]{3,2,1,0:T(8,128)S(1)}, f32[2,28,64,64]{3,2,1,0:T(8,128)}, u32[]{:S(2)}) copy-start(f32[2,28,64,64]{3,2,1,0:T(8,128)} %param.37) | copy-start | bytes 2752516
  59.7 13.7 %copy-start.12 = (f32[4,1792]{1,0:T(4,128)S(1)}, f32[4,1792]{1,0:T(4,128)}, u32[]{:S(2)}) copy-start(f32[4,1792]{1,0:T(4,128)} %wx_ref) | copy-start | bytes 86020
  59.7 13.7 %copy-start.13 = (f32[4,128]{1,0:T(4,128)S(1)}, f32[4,128]{1,0:T(4,128)}, u32[]{:S(2)}) copy-start(f32[4,128]{1,0:T(4,128)} %wb_ref) | copy-start | bytes 6148
  59.7 13.7 %copy-start.14 = (f32[128]{0:T(128)S(1)}, f32[128]{0:T(128)}, u32[]{:S(2)}) copy-start(f32[128]{0:T(128)} %param.33) | copy-start | bytes 1540
  71.2 1.0 copy-start.8
  72.2 1.0 copy-start.10
  73.4 8.4 %copy-start.9 = (bf16[256,2048]{1,0:T(8,128)(2,1)S(1)}, bf16[256,2048]{1,0:T(8,128)(2,1)}, u32[]{:S(2)}) copy-start(bf16[256,2048]{1,0:T(8,128)(2,1)} %copy-done.8) | copy-start | bytes 3145732
  73.4 9.8 %copy-start.11 = (bf16[256,2048]{1,0:T(8,128)(2,1)S(1)}, bf16[256,2048]{1,0:T(8,128)(2,1)}, u32[]{:S(2)}) copy-start(bf16[256,2048]{1,0:T(8,128)(2,1)} %copy-done.10) | copy-start | bytes 3145732
  81.8 24.9 %collective-permute-start.14 = (bf16[256,2048]{1,0:T(8,128)(2,1)S(1)}, bf16[256,2048]{1,0:T(8,128)(2,1)S(1)}, u32[]{:S(2)}, u32[]{:S(2)}) collective-permute-start(bf16[256,2048]{1,0:T(8,128)(2,1)S(1)} %copy-done.9), channel_id=1, source_target_pairs={{0,32},{4,36},{8,40},{12,44},{16,48},{20,52},{24,56},{28,60},{32,0... | collective-permute-start | bytes 3145736 | tf_op jit(solution)/shard_map/ppermute | solution.py:34
  83.2 23.5 %collective-permute-start.19 = (bf16[256,2048]{1,0:T(8,128)(2,1)S(1)}, bf16[256,2048]{1,0:T(8,128)(2,1)S(1)}, u32[]{:S(2)}, u32[]{:S(2)}) collective-permute-start(bf16[256,2048]{1,0:T(8,128)(2,1)S(1)} %copy-done.11), channel_id=1, source_target_pairs={{0,8},{4,12},{8,0},{12,4},{16,24},{20,28},{24,16},{28,20},{32,40},... | collective-permute-start | bytes 3145736 | tf_op jit(solution)/shard_map/ppermute | solution.py:34
  103.5 24.5 %collective-permute-start.13 = (bf16[256,2048]{1,0:T(8,128)(2,1)}, bf16[256,2048]{1,0:T(8,128)(2,1)}, u32[]{:S(2)}, u32[]{:S(2)}) collective-permute-start(bf16[256,2048]{1,0:T(8,128)(2,1)} %get-tuple-element.76), channel_id=1, source_target_pairs={{0,48},{4,52},{8,56},{12,60},{16,0},{20,4},{24,8},{28,12},{32,16},... | collective-permute-start | bytes 3145736 | tf_op jit(solution)/shard_map/ppermute | solution.py:34
  104.7 26.8 %collective-permute-start.12 = (bf16[256,2048]{1,0:T(8,128)(2,1)}, bf16[256,2048]{1,0:T(8,128)(2,1)}, u32[]{:S(2)}, u32[]{:S(2)}) collective-permute-start(bf16[256,2048]{1,0:T(8,128)(2,1)} %get-tuple-element.75), channel_id=1, source_target_pairs={{0,16},{4,20},{8,24},{12,28},{16,32},{20,36},{24,40},{28,44},{32,4... | collective-permute-start | bytes 3145736 | tf_op jit(solution)/shard_map/ppermute | solution.py:34
  105.5 33.8 %collective-permute-start.18 = (bf16[256,2048]{1,0:T(8,128)(2,1)}, bf16[256,2048]{1,0:T(8,128)(2,1)S(1)}, u32[]{:S(2)}, u32[]{:S(2)}) collective-permute-start(bf16[256,2048]{1,0:T(8,128)(2,1)} %get-tuple-element.83), channel_id=1, source_target_pairs={{0,4},{4,8},{8,12},{12,0},{16,20},{20,24},{24,28},{28,16},{32,36},... | collective-permute-start | bytes 3145736 | tf_op jit(solution)/shard_map/ppermute | solution.py:34
  106.7 32.6 %copy-start.16 = (bf16[256,2048]{1,0:T(8,128)(2,1)}, bf16[256,2048]{1,0:T(8,128)(2,1)S(1)}, u32[]{:S(2)}) copy-start(bf16[256,2048]{1,0:T(8,128)(2,1)S(1)} %collective-permute-done.19.refs_3_) | copy-start | bytes 3145732
  106.7 1.1 copy-start.18
  107.8 31.5 %collective-permute-start.20 = (bf16[256,2048]{1,0:T(8,128)(2,1)}, bf16[256,2048]{1,0:T(8,128)(2,1)}, u32[]{:S(2)}, u32[]{:S(2)}) collective-permute-start(bf16[256,2048]{1,0:T(8,128)(2,1)} %get-tuple-element.86), channel_id=1, source_target_pairs={{0,12},{4,0},{8,4},{12,8},{16,28},{20,16},{24,20},{28,24},{32,44},... | collective-permute-start | bytes 3145736 | tf_op jit(solution)/shard_map/ppermute | solution.py:34
  109.8 34.5 %all-to-all-start.1 = ((bf16[16,64,256]{2,1,0:T(8,128)(2,1)}), bf16[16,64,256]{2,1,0:T(8,128)(2,1)S(1)}, u32[]{:S(2)}, u32[]{:S(2)}) async-start(bf16[16,64,256]{2,1,0:T(8,128)(2,1)} %bitcast.10), calls=%async_computation.1 | async-start | bytes 1048576 | tf_op jit(solution)/shard_map/all_to_all | solution.py:506
  135.5 12.1 %collective-permute-start.15 = (bf16[64,2048]{1,0:T(8,128)(2,1)}, bf16[64,2048]{1,0:T(8,128)(2,1)S(1)}, u32[]{:S(2)}, u32[]{:S(2)}) collective-permute-start(bf16[64,2048]{1,0:T(8,128)(2,1)} %get-tuple-element.78), channel_id=1, source_target_pairs={{0,4},{4,8},{8,12},{12,0},{16,20},{20,24},{24,28},{28,16},{32,36},... | collective-permute-start | bytes 786440 | tf_op jit(solution)/shard_map/ppermute | solution.py:34
  135.5 13.1 %collective-permute-start.16 = (bf16[64,2048]{1,0:T(8,128)(2,1)}, bf16[64,2048]{1,0:T(8,128)(2,1)S(1)}, u32[]{:S(2)}, u32[]{:S(2)}) collective-permute-start(bf16[64,2048]{1,0:T(8,128)(2,1)} %get-tuple-element.79), channel_id=1, source_target_pairs={{0,12},{4,0},{8,4},{12,8},{16,28},{20,16},{24,20},{28,24},{32,44},... | collective-permute-start | bytes 786440 | tf_op jit(solution)/shard_map/ppermute | solution.py:34
  138.7 9.9 %collective-permute-start.17 = (bf16[64,2048]{1,0:T(8,128)(2,1)}, bf16[64,2048]{1,0:T(8,128)(2,1)S(1)}, u32[]{:S(2)}, u32[]{:S(2)}) collective-permute-start(bf16[64,2048]{1,0:T(8,128)(2,1)} %get-tuple-element.80), channel_id=1, source_target_pairs={{0,8},{4,12},{8,0},{12,4},{16,24},{20,28},{24,16},{28,20},{32,40},... | collective-permute-start | bytes 786440 | tf_op jit(solution)/shard_map/ppermute | solution.py:34
  139.3 1.0 copy-start.17
  144.3 7.9 %collective-permute-start.21 = (bf16[64,2048]{1,0:T(8,128)(2,1)}, bf16[64,2048]{1,0:T(8,128)(2,1)S(1)}, u32[]{:S(2)}, u32[]{:S(2)}) collective-permute-start(bf16[64,2048]{1,0:T(8,128)(2,1)} %get-tuple-element.93), channel_id=1, source_target_pairs={{0,16},{4,20},{8,24},{12,28},{16,32},{20,36},{24,40},{28,44},{32,4... | collective-permute-start | bytes 786440 | tf_op jit(solution)/shard_map/ppermute | solution.py:34
  144.7 10.0 %collective-permute-start.22 = (bf16[64,2048]{1,0:T(8,128)(2,1)}, bf16[64,2048]{1,0:T(8,128)(2,1)S(1)}, u32[]{:S(2)}, u32[]{:S(2)}) collective-permute-start(bf16[64,2048]{1,0:T(8,128)(2,1)} %get-tuple-element.94), channel_id=1, source_target_pairs={{0,48},{4,52},{8,56},{12,60},{16,0},{20,4},{24,8},{28,12},{32,16},... | collective-permute-start | bytes 786440 | tf_op jit(solution)/shard_map/ppermute | solution.py:34
  147.6 8.1 %collective-permute-start.23 = (bf16[64,2048]{1,0:T(8,128)(2,1)}, bf16[64,2048]{1,0:T(8,128)(2,1)S(1)}, u32[]{:S(2)}, u32[]{:S(2)}) collective-permute-start(bf16[64,2048]{1,0:T(8,128)(2,1)} %get-tuple-element.95), channel_id=1, source_target_pairs={{0,32},{4,36},{8,40},{12,44},{16,48},{20,52},{24,56},{28,60},{32,0... | collective-permute-start | bytes 786440 | tf_op jit(solution)/shard_map/ppermute | solution.py:34
  155.7 1.0 copy-start.2
  156.6 0.9 copy-start.3
where the time goes:
time: 161 us; the launch traced here: 160 us
  Pallas kernels  71.4 us (44%)
  starting transfers between devices  44.9 us (28%)
  waiting for transfers between devices  32.2 us (20%)
  local copies, waits for them, and re-layouts  10.7 us (7%)
    pallas_call x3, Pallas kernels, attend(): pl.pallas_call(functools.partial(attend_kernel, requests, groups, raw is...  49.5 us
    ppermute x24, starting transfers between devices, shifted(): return lax.ppermute(value, 'ctx', pairs)  33.2 us
    ppermute x24, waiting for transfers between devices, shifted(): return lax.ppermute(value, 'ctx', pairs)  32.2 us
    unnamed x51, local copies, waits for them, and re-layouts  9.57 us
    pallas_call x1, Pallas kernels, state_space(): pl.pallas_call(scan_kernel, grid_spec=pltpu.PrefetchScalarGridSpec(num_sc...  8.39 us
    pallas_call x2, Pallas kernels, merge(): pl.pallas_call(merge_kernel, grid=(steps,), in_specs=[spec] * 4, out_spec...  8.1 us
    all_to_all x1, starting transfers between devices, channels_in(): lax.all_to_all(packed, 'ctx', 0, 0, tiled=True)  6.91 us
    all_to_all x1, starting transfers between devices, per_device(): back = lax.all_to_all(after(scanned, one0), 'ctx', 0, 0, tiled=True)  4.73 us
  transfers between devices with their start and end apart: 26, of which 9 were waited for; matrix products, arithmetic and copies ran while one was open for 1% of the time, Pallas kernels for 42%

commit v1 on v0

--- a/solution.py
+++ b/solution.py
@@ -44,7 +44,7 @@
     return jnp.concatenate([block, extra], axis=1)
 
 
-def pad_cache(info, request, k_ref, gk_ref, v_ref, gv_ref, ko_ref, vo_ref):
+def pad_cache(info, request, k_ref, gk_ref, v_ref, gv_ref, ko_ref, vo_ref, h):
     rows = k_ref.shape[1]
     group_rows = gk_ref.shape[1]
     first = lax.axis_index("ctx") * rows
@@ -54,12 +54,11 @@
     cache_bias = jnp.where((lane == 0) & (first + row >= length), NEG_FILL, 0.0).astype(BF)
     group_bias = jnp.zeros((group_rows, PAD - HD), BF)
     ones = jnp.where(lane == 0, 1.0, 0.0).astype(BF)
-    for h in range(ko_ref.shape[1]):
-        window = slice(h * HD, (h + 1) * HD)
-        ko_ref[0, h, :rows, :] = widened(k_ref[0, :, window], cache_bias)
-        ko_ref[0, h, rows:, :] = widened(gk_ref[0, :, window], group_bias)
-        vo_ref[0, h, :rows, :] = widened(v_ref[0, :, window], ones)
-        vo_ref[0, h, rows:, :] = widened(gv_ref[0, :, window], ones[:group_rows])
+    window = slice(h * HD, (h + 1) * HD)
+    ko_ref[0, h, :rows, :] = widened(k_ref[0, :, window], cache_bias)
+    ko_ref[0, h, rows:, :] = widened(gk_ref[0, :, window], group_bias)
+    vo_ref[0, h, :rows, :] = widened(v_ref[0, :, window], ones)
+    vo_ref[0, h, rows:, :] = widened(gv_ref[0, :, window], ones[:group_rows])
 
 
 def attend_kernel(requests, groups, pads, info, *refs):
@@ -78,8 +77,6 @@
     block = 64
     cached = k_ref.shape[2] - block
     scale = math.log2(math.e) / math.sqrt(HD)
-    if pads:
-        pad_cache(info, turn, *raw, k_ref, v_ref)
     position = lax.axis_index("ctx")
 
     def body(n):
@@ -96,6 +93,8 @@
         mine = q_refs[n * sets : (n + 1) * sets]
 
         def scored(i):
+            if pads:
+                pad_cache(info, requests[n], *raw, k_ref, v_ref, i)
             queries = [ref[:, i * PAD : (i + 1) * PAD] for ref in mine]
             return lax.dot_general(
                 jnp.concatenate(queries, axis=0) if sets > 1 else queries[0],

time: 161 us -> 161 us (level)
  no operation moved by 1% of the time
where the time goes in v1:
time: 161 us; the launch traced here: 160 us
  Pallas kernels  71.4 us (44%)
  starting transfers between devices  44.9 us (28%)
  waiting for transfers between devices  32.2 us (20%)
  local copies, waits for them, and re-layouts  10.7 us (7%)
    pallas_call x3, Pallas kernels, attend(): pl.pallas_call(functools.partial(attend_kernel, requests, groups, raw is...  49.5 us
    ppermute x24, starting transfers between devices, shifted(): return lax.ppermute(value, 'ctx', pairs)  33.3 us
    ppermute x24, waiting for transfers between devices, shifted(): return lax.ppermute(value, 'ctx', pairs)  32.2 us
    unnamed x51, local copies, waits for them, and re-layouts  9.57 us
    pallas_call x1, Pallas kernels, state_space(): pl.pallas_call(scan_kernel, grid_spec=pltpu.PrefetchScalarGridSpec(num_sc...  8.39 us
    pallas_call x2, Pallas kernels, merge(): pl.pallas_call(merge_kernel, grid=(steps,), in_specs=[spec] * 4, out_spec...  8.1 us
    all_to_all x1, starting transfers between devices, channels_in(): lax.all_to_all(packed, 'ctx', 0, 0, tiled=True)  6.91 us
    all_to_all x1, starting transfers between devices, per_device(): back = lax.all_to_all(after(scanned, one0), 'ctx', 0, 0, tiled=True)  4.72 us
  transfers between devices with their start and end apart: 26, of which 9 were waited for; matrix products, arithmetic and copies ran while one was open for 1% of the time, Pallas kernels for 42%

profile of v1, /device:TPU:0, one launch (start us, length us, event | category | flops | bytes accessed | tf_op | source)
XLA Modules:
  0.0 160.3 jit_solution(14596019404453185074)
XLA Ops:
  0.6 1.1 slice_bitcast_fusion
  1.7 2.9 %collective-permute-start = (bf16[64,1792]{1,0:T(8,128)(2,1)S(1)}, bf16[64,1792]{1,0:T(8,128)(2,1)S(1)}, u32[]{:S(2)}, u32[]{:S(2)}) collective-permute-start(bf16[64,1792]{1,0:T(8,128)(2,1)S(1)} %get-tuple-element.97), channel_id=1, source_target_pairs={{0,12},{4,0},{8,4},{12,8},{16,28},{20,16},{24,20},{28,24},{32,44},... | collective-permute-start | bytes 688136 | tf_op jit(solution)/shard_map/ppermute | solution.py:34
  4.6 1.6 collective-permute-start.5
  6.2 2.9 %collective-permute-start.4 = (bf16[64,1792]{1,0:T(8,128)(2,1)S(1)}, bf16[64,1792]{1,0:T(8,128)(2,1)S(1)}, u32[]{:S(2)}, u32[]{:S(2)}) collective-permute-start(bf16[64,1792]{1,0:T(8,128)(2,1)S(1)} %get-tuple-element.96), channel_id=1, source_target_pairs={{0,32},{4,36},{8,40},{12,44},{16,48},{20,52},{24,56},{28,60},{32,0... | collective-permute-start | bytes 688136 | tf_op jit(solution)/shard_map/ppermute | solution.py:34
  9.1 1.3 collective-permute-start.3
  10.5 2.3 %collective-permute-start.1 = (bf16[64,1792]{1,0:T(8,128)(2,1)S(1)}, bf16[64,1792]{1,0:T(8,128)(2,1)S(1)}, u32[]{:S(2)}, u32[]{:S(2)}) collective-permute-start(bf16[64,1792]{1,0:T(8,128)(2,1)S(1)} %get-tuple-element.97), channel_id=1, source_target_pairs={{0,8},{4,12},{8,0},{12,4},{16,24},{20,28},{24,16},{28,20},{32,40},... | collective-permute-start | bytes 688136 | tf_op jit(solution)/shard_map/ppermute | solution.py:34
  12.7 0.8 copy.21.dt_ref
  13.6 1.0 copy-done.1
  14.6 0.8 copy-done.4
  15.4 1.1 pack.1
  16.5 2.6 %collective-permute-done.4.refs_4_ = bf16[64,1792]{1,0:T(8,128)(2,1)S(1)} collective-permute-done((bf16[64,1792]{1,0:T(8,128)(2,1)S(1)}, bf16[64,1792]{1,0:T(8,128)(2,1)S(1)}, u32[]{:S(2)}, u32[]{:S(2)}) %collective-permute-start.4) | collective-permute-done | bytes 229408 | tf_op jit(solution)/shard_map/ppermute | solution.py:34
  19.1 3.7 %collective-permute-done.2.refs_2_ = bf16[64,1792]{1,0:T(8,128)(2,1)S(1)} collective-permute-done((bf16[64,1792]{1,0:T(8,128)(2,1)S(1)}, bf16[64,1792]{1,0:T(8,128)(2,1)S(1)}, u32[]{:S(2)}, u32[]{:S(2)}) %collective-permute-start.2) | collective-permute-done | bytes 229408 | tf_op jit(solution)/shard_map/ppermute | solution.py:34
  22.8 1.0 copy-done
  23.8 0.7 join.1
  24.5 0.5 collective-permute-start.6
  25.0 0.6 collective-permute-start.7
  25.6 0.1 pad_add_fusion.info
  25.6 6.9 %all-to-all-start = ((bf16[16,64,384]{2,1,0:T(8,128)(2,1)}), bf16[16,64,384]{2,1,0:T(8,128)(2,1)S(1)}, u32[]{:S(2)}, u32[]{:S(2)}) async-start(bf16[16,64,384]{2,1,0:T(8,128)(2,1)} %pack.1), calls=%async_computation | async-start | bytes 1572864 | tf_op jit(solution)/shard_map/all_to_all | solution.py:414
  32.6 0.0 copy-start.15
  32.6 19.2 %attend.3 = (bf16[256,2048]{1,0:T(8,128)(2,1)}, bf16[256,2048]{1,0:T(8,128)(2,1)}, bf16[2,8,1088,256]{3,2,1,0:T(8,128)(2,1)}, bf16[2,8,1088,256]{3,2,1,0:T(8,128)(2,1)}) custom-call(s32[2]{0:T(128)} %info.3, bf16[256,2048]{1,0:T(8,128)(2,1)} %copy-done.7, bf16[256,2048]{1,0:T(8,128)(2,1)} %copy-done.6, bf16[2,1024,1792]{2,1,0:T(8,128)(2,1)} %refs_2_.1, ...), custom_call_target="tpu_custom_call" | custom-call | flops 6845104128 | bytes 40291456 | tf_op jit(solution)/shard_map/attend/pallas_call | solution.py:168
  51.8 1.3 collective-permute-done.6.refs_0_
  53.1 0.7 collective-permute-start.9
  53.8 2.5 %collective-permute-start.8 = (bf16[256,2048]{1,0:T(8,128)(2,1)}, bf16[256,2048]{1,0:T(8,128)(2,1)}, u32[]{:S(2)}, u32[]{:S(2)}) collective-permute-start(bf16[256,2048]{1,0:T(8,128)(2,1)} %copy-done.7), channel_id=1, source_target_pairs={{0,48},{4,52},{8,56},{12,60},{16,0},{20,4},{24,8},{28,12},{32,16},... | collective-permute-start | bytes 3145736 | tf_op jit(solution)/shard_map/ppermute | solution.py:34
  56.4 0.7 collective-permute-start.11
  57.1 2.5 %collective-permute-start.10 = (bf16[256,2048]{1,0:T(8,128)(2,1)}, bf16[256,2048]{1,0:T(8,128)(2,1)}, u32[]{:S(2)}, u32[]{:S(2)}) collective-permute-start(bf16[256,2048]{1,0:T(8,128)(2,1)} %copy-done.6), channel_id=1, source_target_pairs={{0,12},{4,0},{8,4},{12,8},{16,28},{20,16},{24,20},{28,24},{32,44},... | collective-permute-start | bytes 3145736 | tf_op jit(solution)/shard_map/ppermute | solution.py:34
  59.6 0.0 copy-start.22
  59.6 0.0 copy-start.23
  59.6 0.0 copy-start.24
  59.6 0.0 copy-start.5
  59.7 0.0 copy-start.12
  59.7 0.0 copy-start.13
  59.7 0.0 copy-start.14
  59.7 11.5 %attend.4 = (bf16[256,2048]{1,0:T(8,128)(2,1)S(1)}, bf16[256,2048]{1,0:T(8,128)(2,1)S(1)}) custom-call(s32[2]{0:T(128)S(1)} %copy-done.15, bf16[256,2048]{1,0:T(8,128)(2,1)} %collective-permute-done.6.refs_0_, bf16[256,2048]{1,0:T(8,128)(2,1)} %collective-permute-done.7.refs_1_, bf16[2,8,1088,256]{3,2,1,0:T(8,128)(2,1)} %get-tuple-element.55.refs_2_.refs_4_, ...), custom_call_target="tpu_custom_call" | custom-call | flops 6845104128 | bytes 24291456 | tf_op jit(solution)/shard_map/attend/pallas_call | solution.py:168
  71.2 1.0 copy-done.8
  72.2 1.0 copy-done.10
  73.3 0.1 select_maximum_fusion.head_ref
  73.4 8.4 %scan.1 = bf16[1024,256]{1,0:T(8,128)(2,1)} custom-call(s32[2]{0:T(128)S(1)} %pad_add_fusion.info, bf16[1024,384]{1,0:T(8,128)(2,1)S(1)} %bitcast.13, bf16[2,3,1792]{2,1,0:T(4,128)(2,1)S(1)} %copy.22.cx_ref, f32[4,1792]{1,0:T(4,128)S(1)} %copy-done.12, f32[1,1792]{1,0:T(1,128)S(1)} %broadcast_in_dim.6.bx_ref, bf16[2,3,128]{2,1,0:T(4,128)(2,1)S(1)} %copy.23.cb_ref, ...), custom_call_target="tpu_custom_call" | custom-call | flops 8000000000 | bytes 2500000 | tf_op jit(solution)/shard_map/scan/pallas_call | solution.py:434
  81.8 1.4 collective-permute-start.14
  83.2 1.5 collective-permute-start.19
  84.7 18.7 %attend.5 = (bf16[256,2048]{1,0:T(8,128)(2,1)}, bf16[256,2048]{1,0:T(8,128)(2,1)}, bf16[256,2048]{1,0:T(8,128)(2,1)}, bf16[256,2048]{1,0:T(8,128)(2,1)}) custom-call(s32[2]{0:T(128)} %info.3, bf16[256,2048]{1,0:T(8,128)(2,1)} %collective-permute-done.8.refs_0_, bf16[256,2048]{1,0:T(8,128)(2,1)} %collective-permute-done.9.refs_1_, ...), custom_call_target="tpu_custom_call" | custom-call | flops 13690208256 | bytes 30582912 | tf_op jit(solution)/shard_map/attend/pallas_call | solution.py:168
  103.4 1.2 collective-permute-start.13
  104.6 0.8 collective-permute-start.12
  105.5 0.6 collective-permute-start.18
  106.0 0.6 collective-permute-done.19.refs_3_
  106.7 1.1 copy-done.18
  107.7 2.1 %collective-permute-start.20 = (bf16[256,2048]{1,0:T(8,128)(2,1)}, bf16[256,2048]{1,0:T(8,128)(2,1)}, u32[]{:S(2)}, u32[]{:S(2)}) collective-permute-start(bf16[256,2048]{1,0:T(8,128)(2,1)} %get-tuple-element.86), channel_id=1, source_target_pairs={{0,12},{4,0},{8,4},{12,8},{16,28},{20,16},{24,20},{28,24},{32,44},... | collective-permute-start | bytes 3145736 | tf_op jit(solution)/shard_map/ppermute | solution.py:34
  109.8 4.7 %all-to-all-start.1 = ((bf16[16,64,256]{2,1,0:T(8,128)(2,1)}), bf16[16,64,256]{2,1,0:T(8,128)(2,1)S(1)}, u32[]{:S(2)}, u32[]{:S(2)}) async-start(bf16[16,64,256]{2,1,0:T(8,128)(2,1)} %bitcast.10), calls=%async_computation.1 | async-start | bytes 1048576 | tf_op jit(solution)/shard_map/all_to_all | solution.py:505
  114.5 13.4 %collective-permute-done.13.refs_2_ = bf16[256,2048]{1,0:T(8,128)(2,1)} collective-permute-done((bf16[256,2048]{1,0:T(8,128)(2,1)}, bf16[256,2048]{1,0:T(8,128)(2,1)}, u32[]{:S(2)}, u32[]{:S(2)}) %collective-permute-start.13) | collective-permute-done | bytes 1048608 | tf_op jit(solution)/shard_map/ppermute | solution.py:34
  127.9 3.4 %collective-permute-done.12.refs_1_ = bf16[256,2048]{1,0:T(8,128)(2,1)} collective-permute-done((bf16[256,2048]{1,0:T(8,128)(2,1)}, bf16[256,2048]{1,0:T(8,128)(2,1)}, u32[]{:S(2)}, u32[]{:S(2)}) %collective-permute-start.12) | collective-permute-done | bytes 1048608 | tf_op jit(solution)/shard_map/ppermute | solution.py:34
  131.4 4.0 %merge.2 = (bf16[64,2048]{1,0:T(8,128)(2,1)}, bf16[64,2048]{1,0:T(8,128)(2,1)}, bf16[64,2048]{1,0:T(8,128)(2,1)}, bf16[64,2048]{1,0:T(8,128)(2,1)}) custom-call(bf16[256,2048]{1,0:T(8,128)(2,1)} %get-tuple-element.69.refs_0_, bf16[256,2048]{1,0:T(8,128)(2,1)} %collective-permute-done.12.refs_1_, bf16[256,2048]{1,0:T(8,128)(2,1)} %collective-permute-done.13.refs_2_, ...), custom_call_target="tpu_custom_call" | custom-call | flops 4194304 | bytes 5242880 | tf_op jit(solution)/shard_map/merge/pallas_call | solution.py:232
  135.4 0.0 collective-permute-start.15
  135.4 3.2 %collective-permute-start.16 = (bf16[64,2048]{1,0:T(8,128)(2,1)}, bf16[64,2048]{1,0:T(8,128)(2,1)S(1)}, u32[]{:S(2)}, u32[]{:S(2)}) collective-permute-start(bf16[64,2048]{1,0:T(8,128)(2,1)} %get-tuple-element.79), channel_id=1, source_target_pairs={{0,12},{4,0},{8,4},{12,8},{16,28},{20,16},{24,20},{28,24},{32,44},... | collective-permute-start | bytes 786440 | tf_op jit(solution)/shard_map/ppermute | solution.py:34
  138.6 0.6 collective-permute-start.17
  139.3 1.0 copy-done.17
  140.2 4.1 %merge.3 = (bf16[64,2048]{1,0:T(8,128)(2,1)}, bf16[64,2048]{1,0:T(8,128)(2,1)}, bf16[64,2048]{1,0:T(8,128)(2,1)}, bf16[64,2048]{1,0:T(8,128)(2,1)}) custom-call(bf16[256,2048]{1,0:T(8,128)(2,1)} %get-tuple-element.82.refs_0_, bf16[256,2048]{1,0:T(8,128)(2,1)} %copy-done.17, bf16[256,2048]{1,0:T(8,128)(2,1)} %collective-permute-done.20.refs_2_, ...), custom_call_target="tpu_custom_call" | custom-call | flops 4194304 | bytes 5242880 | tf_op jit(solution)/shard_map/merge/pallas_call | solution.py:232
  144.3 0.3 collective-permute-start.21
  144.6 3.0 %collective-permute-start.22 = (bf16[64,2048]{1,0:T(8,128)(2,1)}, bf16[64,2048]{1,0:T(8,128)(2,1)S(1)}, u32[]{:S(2)}, u32[]{:S(2)}) collective-permute-start(bf16[64,2048]{1,0:T(8,128)(2,1)} %get-tuple-element.94), channel_id=1, source_target_pairs={{0,48},{4,52},{8,56},{12,60},{16,0},{20,4},{24,8},{28,12},{32,16},... | collective-permute-start | bytes 786440 | tf_op jit(solution)/shard_map/ppermute | solution.py:34
  147.6 0.9 unpack.1
  148.6 3.6 %collective-permute-done.21.refs_5_ = bf16[64,2048]{1,0:T(8,128)(2,1)S(1)} collective-permute-done((bf16[64,2048]{1,0:T(8,128)(2,1)}, bf16[64,2048]{1,0:T(8,128)(2,1)S(1)}, u32[]{:S(2)}, u32[]{:S(2)}) %collective-permute-start.21) | collective-permute-done | bytes 262176 | tf_op jit(solution)/shard_map/ppermute | solution.py:34
  152.2 2.5 %collective-permute-done.22.refs_6_ = bf16[64,2048]{1,0:T(8,128)(2,1)S(1)} collective-permute-done((bf16[64,2048]{1,0:T(8,128)(2,1)}, bf16[64,2048]{1,0:T(8,128)(2,1)S(1)}, u32[]{:S(2)}, u32[]{:S(2)}) %collective-permute-start.22) | collective-permute-done | bytes 262176 | tf_op jit(solution)/shard_map/ppermute | solution.py:34
  154.6 1.1 collective-permute-done.23.refs_7_
  155.7 0.9 copy-done.2
  156.6 0.9 copy-done.3
  157.6 2.7 %finish.1 = bf16[2,64,1792]{2,1,0:T(8,128)(2,1)} custom-call(bf16[64,2048]{1,0:T(8,128)(2,1)S(1)} %copy-done.2, bf16[64,2048]{1,0:T(8,128)(2,1)S(1)} %collective-permute-done.15.refs_1_, bf16[64,2048]{1,0:T(8,128)(2,1)S(1)} %collective-permute-done.16.refs_2_, bf16[64,2048]{1,0:T(8,128)(2,1)S(1)} %collective-permute-done.17.refs_3_, ...), custom_call_target="tpu_custom_call" | custom-call | flops 2097152 | bytes 2621440 | tf_op jit(solution)/shard_map/finish/pallas_call | solution.py:261
  (55 shorter events, 0.1 us)
Async XLA Ops:
  1.7 8.7 %collective-permute-start = (bf16[64,1792]{1,0:T(8,128)(2,1)S(1)}, bf16[64,1792]{1,0:T(8,128)(2,1)S(1)}, u32[]{:S(2)}, u32[]{:S(2)}) collective-permute-start(bf16[64,1792]{1,0:T(8,128)(2,1)S(1)} %get-tuple-element.97), channel_id=1, source_target_pairs={{0,12},{4,0},{8,4},{12,8},{16,28},{20,16},{24,20},{28,24},{32,44},... | collective-permute-start | bytes 688136 | tf_op jit(solution)/shard_map/ppermute | solution.py:34
  4.6 11.9 %collective-permute-start.5 = (bf16[64,1792]{1,0:T(8,128)(2,1)S(1)}, bf16[64,1792]{1,0:T(8,128)(2,1)S(1)}, u32[]{:S(2)}, u32[]{:S(2)}) collective-permute-start(bf16[64,1792]{1,0:T(8,128)(2,1)S(1)} %get-tuple-element.96), channel_id=1, source_target_pairs={{0,16},{4,20},{8,24},{12,28},{16,32},{20,36},{24,40},{28,44},{32,4... | collective-permute-start | bytes 688136 | tf_op jit(solution)/shard_map/ppermute | solution.py:34
  6.2 12.9 %collective-permute-start.4 = (bf16[64,1792]{1,0:T(8,128)(2,1)S(1)}, bf16[64,1792]{1,0:T(8,128)(2,1)S(1)}, u32[]{:S(2)}, u32[]{:S(2)}) collective-permute-start(bf16[64,1792]{1,0:T(8,128)(2,1)S(1)} %get-tuple-element.96), channel_id=1, source_target_pairs={{0,32},{4,36},{8,40},{12,44},{16,48},{20,52},{24,56},{28,60},{32,0... | collective-permute-start | bytes 688136 | tf_op jit(solution)/shard_map/ppermute | solution.py:34
  9.1 10.0 %collective-permute-start.3 = (bf16[64,1792]{1,0:T(8,128)(2,1)S(1)}, bf16[64,1792]{1,0:T(8,128)(2,1)S(1)}, u32[]{:S(2)}, u32[]{:S(2)}) collective-permute-start(bf16[64,1792]{1,0:T(8,128)(2,1)S(1)} %get-tuple-element.96), channel_id=1, source_target_pairs={{0,48},{4,52},{8,56},{12,60},{16,0},{20,4},{24,8},{28,12},{32,16},... | collective-permute-start | bytes 688136 | tf_op jit(solution)/shard_map/ppermute | solution.py:34
  10.5 12.3 %collective-permute-start.2 = (bf16[64,1792]{1,0:T(8,128)(2,1)S(1)}, bf16[64,1792]{1,0:T(8,128)(2,1)S(1)}, u32[]{:S(2)}, u32[]{:S(2)}) collective-permute-start(bf16[64,1792]{1,0:T(8,128)(2,1)S(1)} %get-tuple-element.97), channel_id=1, source_target_pairs={{0,4},{4,8},{8,12},{12,0},{16,20},{20,24},{24,28},{28,16},{32,36},... | collective-permute-start | bytes 688136 | tf_op jit(solution)/shard_map/ppermute | solution.py:34
  10.5 12.3 %collective-permute-start.1 = (bf16[64,1792]{1,0:T(8,128)(2,1)S(1)}, bf16[64,1792]{1,0:T(8,128)(2,1)S(1)}, u32[]{:S(2)}, u32[]{:S(2)}) collective-permute-start(bf16[64,1792]{1,0:T(8,128)(2,1)S(1)} %get-tuple-element.97), channel_id=1, source_target_pairs={{0,8},{4,12},{8,0},{12,4},{16,24},{20,28},{24,16},{28,20},{32,40},... | collective-permute-start | bytes 688136 | tf_op jit(solution)/shard_map/ppermute | solution.py:34
  13.6 1.0 copy-start.1
  14.6 0.8 copy-start.4
  22.8 1.0 copy-start
  24.5 8.1 %copy-start.6 = (bf16[256,2048]{1,0:T(8,128)(2,1)}, bf16[256,2048]{1,0:T(8,128)(2,1)S(1)}, u32[]{:S(2)}) copy-start(bf16[256,2048]{1,0:T(8,128)(2,1)S(1)} %get-tuple-element.72.refs_1_) | copy-start | bytes 3145732
  24.5 8.1 %copy-start.7 = (bf16[256,2048]{1,0:T(8,128)(2,1)}, bf16[256,2048]{1,0:T(8,128)(2,1)S(1)}, u32[]{:S(2)}) copy-start(bf16[256,2048]{1,0:T(8,128)(2,1)S(1)} %get-tuple-element.71.refs_0_) | copy-start | bytes 3145732
  24.5 28.6 %collective-permute-start.6 = (bf16[256,2048]{1,0:T(8,128)(2,1)S(1)}, bf16[256,2048]{1,0:T(8,128)(2,1)}, u32[]{:S(2)}, u32[]{:S(2)}) collective-permute-start(bf16[256,2048]{1,0:T(8,128)(2,1)S(1)} %get-tuple-element.71.refs_0_), channel_id=1, source_target_pairs={{0,32},{4,36},{8,40},{12,44},{16,48},{20,52},{24,56},{28,60},{32,0... | collective-permute-start | bytes 3145736 | tf_op jit(solution)/shard_map/ppermute | solution.py:34
  25.0 28.1 %collective-permute-start.7 = (bf16[256,2048]{1,0:T(8,128)(2,1)S(1)}, bf16[256,2048]{1,0:T(8,128)(2,1)}, u32[]{:S(2)}, u32[]{:S(2)}) collective-permute-start(bf16[256,2048]{1,0:T(8,128)(2,1)S(1)} %get-tuple-element.72.refs_1_), channel_id=1, source_target_pairs={{0,8},{4,12},{8,0},{12,4},{16,24},{20,28},{24,16},{28,20},{32,40},... | collective-permute-start | bytes 3145736 | tf_op jit(solution)/shard_map/ppermute | solution.py:34
  25.6 47.5 %all-to-all-start = ((bf16[16,64,384]{2,1,0:T(8,128)(2,1)}), bf16[16,64,384]{2,1,0:T(8,128)(2,1)S(1)}, u32[]{:S(2)}, u32[]{:S(2)}) async-start(bf16[16,64,384]{2,1,0:T(8,128)(2,1)} %pack.1), calls=%async_computation | async-start | bytes 1572864 | tf_op jit(solution)/shard_map/all_to_all | solution.py:414
  32.6 27.0 %copy-start.15 = (s32[2]{0:T(128)S(1)}, s32[2]{0:T(128)}, u32[]{:S(2)}) copy-start(s32[2]{0:T(128)} %info.3) | copy-start | bytes 28
  53.1 28.7 %collective-permute-start.9 = (bf16[256,2048]{1,0:T(8,128)(2,1)}, bf16[256,2048]{1,0:T(8,128)(2,1)}, u32[]{:S(2)}, u32[]{:S(2)}) collective-permute-start(bf16[256,2048]{1,0:T(8,128)(2,1)} %copy-done.7), channel_id=1, source_target_pairs={{0,16},{4,20},{8,24},{12,28},{16,32},{20,36},{24,40},{28,44},{32,4... | collective-permute-start | bytes 3145736 | tf_op jit(solution)/shard_map/ppermute | solution.py:34
  53.8 27.9 %collective-permute-start.8 = (bf16[256,2048]{1,0:T(8,128)(2,1)}, bf16[256,2048]{1,0:T(8,128)(2,1)}, u32[]{:S(2)}, u32[]{:S(2)}) collective-permute-start(bf16[256,2048]{1,0:T(8,128)(2,1)} %copy-done.7), channel_id=1, source_target_pairs={{0,48},{4,52},{8,56},{12,60},{16,0},{20,4},{24,8},{28,12},{32,16},... | collective-permute-start | bytes 3145736 | tf_op jit(solution)/shard_map/ppermute | solution.py:34
  56.4 25.4 %collective-permute-start.11 = (bf16[256,2048]{1,0:T(8,128)(2,1)}, bf16[256,2048]{1,0:T(8,128)(2,1)}, u32[]{:S(2)}, u32[]{:S(2)}) collective-permute-start(bf16[256,2048]{1,0:T(8,128)(2,1)} %copy-done.6), channel_id=1, source_target_pairs={{0,4},{4,8},{8,12},{12,0},{16,20},{20,24},{24,28},{28,16},{32,36},... | collective-permute-start | bytes 3145736 | tf_op jit(solution)/shard_map/ppermute | solution.py:34
  57.1 24.7 %collective-permute-start.10 = (bf16[256,2048]{1,0:T(8,128)(2,1)}, bf16[256,2048]{1,0:T(8,128)(2,1)}, u32[]{:S(2)}, u32[]{:S(2)}) collective-permute-start(bf16[256,2048]{1,0:T(8,128)(2,1)} %copy-done.6), channel_id=1, source_target_pairs={{0,12},{4,0},{8,4},{12,8},{16,28},{20,16},{24,20},{28,24},{32,44},... | collective-permute-start | bytes 3145736 | tf_op jit(solution)/shard_map/ppermute | solution.py:34
  59.6 13.6 %copy-start.21 = (bf16[2,3,128]{2,0,1:T(2,128)(2,1)S(1)}, bf16[2,3,128]{2,0,1:T(2,128)(2,1)}, u32[]{:S(2)}) copy-start(bf16[2,3,128]{2,0,1:T(2,128)(2,1)} %param.29) | copy-start | bytes 4612
  59.6 13.6 %copy-start.20 = (f32[1792]{0:T(1024)S(1)}, f32[1792]{0:T(1024)}, u32[]{:S(2)}) copy-start(f32[1792]{0:T(1024)} %param.31) | copy-start | bytes 21508
  59.6 13.6 %copy-start.19 = (bf16[2,3,1792]{2,0,1:T(2,128)(2,1)S(1)}, bf16[2,3,1792]{2,0,1:T(2,128)(2,1)}, u32[]{:S(2)}) copy-start(bf16[2,3,1792]{2,0,1:T(2,128)(2,1)} %param.28) | copy-start | bytes 64516
  59.6 13.6 %copy-start.22 = (f32[28]{0:T(128)S(1)}, f32[28]{0:T(128)}, u32[]{:S(2)}) copy-start(f32[28]{0:T(128)} %param.36) | copy-start | bytes 340
  59.6 13.6 %copy-start.23 = (f32[28]{0:T(128)S(1)}, f32[28]{0:T(128)}, u32[]{:S(2)}) copy-start(f32[28]{0:T(128)} %param.35) | copy-start | bytes 340
  59.6 13.6 %copy-start.24 = (f32[28]{0:T(128)S(1)}, f32[28]{0:T(128)}, u32[]{:S(2)}) copy-start(f32[28]{0:T(128)} %param.34) | copy-start | bytes 340
  59.6 13.7 %copy-start.5 = (f32[2,28,64,64]{3,2,1,0:T(8,128)S(1)}, f32[2,28,64,64]{3,2,1,0:T(8,128)}, u32[]{:S(2)}) copy-start(f32[2,28,64,64]{3,2,1,0:T(8,128)} %param.37) | copy-start | bytes 2752516
  59.7 13.7 %copy-start.12 = (f32[4,1792]{1,0:T(4,128)S(1)}, f32[4,1792]{1,0:T(4,128)}, u32[]{:S(2)}) copy-start(f32[4,1792]{1,0:T(4,128)} %wx_ref) | copy-start | bytes 86020
  59.7 13.7 %copy-start.13 = (f32[4,128]{1,0:T(4,128)S(1)}, f32[4,128]{1,0:T(4,128)}, u32[]{:S(2)}) copy-start(f32[4,128]{1,0:T(4,128)} %wb_ref) | copy-start | bytes 6148
  59.7 13.7 %copy-start.14 = (f32[128]{0:T(128)S(1)}, f32[128]{0:T(128)}, u32[]{:S(2)}) copy-start(f32[128]{0:T(128)} %param.33) | copy-start | bytes 1540
  71.2 1.0 copy-start.8
  72.2 1.0 copy-start.10
  73.4 8.4 %copy-start.9 = (bf16[256,2048]{1,0:T(8,128)(2,1)S(1)}, bf16[256,2048]{1,0:T(8,128)(2,1)}, u32[]{:S(2)}) copy-start(bf16[256,2048]{1,0:T(8,128)(2,1)} %copy-done.8) | copy-start | bytes 3145732
  73.4 9.8 %copy-start.11 = (bf16[256,2048]{1,0:T(8,128)(2,1)S(1)}, bf16[256,2048]{1,0:T(8,128)(2,1)}, u32[]{:S(2)}) copy-start(bf16[256,2048]{1,0:T(8,128)(2,1)} %copy-done.10) | copy-start | bytes 3145732
  81.8 24.9 %collective-permute-start.14 = (bf16[256,2048]{1,0:T(8,128)(2,1)S(1)}, bf16[256,2048]{1,0:T(8,128)(2,1)S(1)}, u32[]{:S(2)}, u32[]{:S(2)}) collective-permute-start(bf16[256,2048]{1,0:T(8,128)(2,1)S(1)} %copy-done.9), channel_id=1, source_target_pairs={{0,32},{4,36},{8,40},{12,44},{16,48},{20,52},{24,56},{28,60},{32,0... | collective-permute-start | bytes 3145736 | tf_op jit(solution)/shard_map/ppermute | solution.py:34
  83.2 23.5 %collective-permute-start.19 = (bf16[256,2048]{1,0:T(8,128)(2,1)S(1)}, bf16[256,2048]{1,0:T(8,128)(2,1)S(1)}, u32[]{:S(2)}, u32[]{:S(2)}) collective-permute-start(bf16[256,2048]{1,0:T(8,128)(2,1)S(1)} %copy-done.11), channel_id=1, source_target_pairs={{0,8},{4,12},{8,0},{12,4},{16,24},{20,28},{24,16},{28,20},{32,40},... | collective-permute-start | bytes 3145736 | tf_op jit(solution)/shard_map/ppermute | solution.py:34
  103.4 24.5 %collective-permute-start.13 = (bf16[256,2048]{1,0:T(8,128)(2,1)}, bf16[256,2048]{1,0:T(8,128)(2,1)}, u32[]{:S(2)}, u32[]{:S(2)}) collective-permute-start(bf16[256,2048]{1,0:T(8,128)(2,1)} %get-tuple-element.76), channel_id=1, source_target_pairs={{0,48},{4,52},{8,56},{12,60},{16,0},{20,4},{24,8},{28,12},{32,16},... | collective-permute-start | bytes 3145736 | tf_op jit(solution)/shard_map/ppermute | solution.py:34
  104.6 26.7 %collective-permute-start.12 = (bf16[256,2048]{1,0:T(8,128)(2,1)}, bf16[256,2048]{1,0:T(8,128)(2,1)}, u32[]{:S(2)}, u32[]{:S(2)}) collective-permute-start(bf16[256,2048]{1,0:T(8,128)(2,1)} %get-tuple-element.75), channel_id=1, source_target_pairs={{0,16},{4,20},{8,24},{12,28},{16,32},{20,36},{24,40},{28,44},{32,4... | collective-permute-start | bytes 3145736 | tf_op jit(solution)/shard_map/ppermute | solution.py:34
  105.5 33.8 %collective-permute-start.18 = (bf16[256,2048]{1,0:T(8,128)(2,1)}, bf16[256,2048]{1,0:T(8,128)(2,1)S(1)}, u32[]{:S(2)}, u32[]{:S(2)}) collective-permute-start(bf16[256,2048]{1,0:T(8,128)(2,1)} %get-tuple-element.83), channel_id=1, source_target_pairs={{0,4},{4,8},{8,12},{12,0},{16,20},{20,24},{24,28},{28,16},{32,36},... | collective-permute-start | bytes 3145736 | tf_op jit(solution)/shard_map/ppermute | solution.py:34
  106.6 32.6 %copy-start.16 = (bf16[256,2048]{1,0:T(8,128)(2,1)}, bf16[256,2048]{1,0:T(8,128)(2,1)S(1)}, u32[]{:S(2)}) copy-start(bf16[256,2048]{1,0:T(8,128)(2,1)S(1)} %collective-permute-done.19.refs_3_) | copy-start | bytes 3145732
  106.7 1.1 copy-start.18
  107.7 31.5 %collective-permute-start.20 = (bf16[256,2048]{1,0:T(8,128)(2,1)}, bf16[256,2048]{1,0:T(8,128)(2,1)}, u32[]{:S(2)}, u32[]{:S(2)}) collective-permute-start(bf16[256,2048]{1,0:T(8,128)(2,1)} %get-tuple-element.86), channel_id=1, source_target_pairs={{0,12},{4,0},{8,4},{12,8},{16,28},{20,16},{24,20},{28,24},{32,44},... | collective-permute-start | bytes 3145736 | tf_op jit(solution)/shard_map/ppermute | solution.py:34
  109.8 34.5 %all-to-all-start.1 = ((bf16[16,64,256]{2,1,0:T(8,128)(2,1)}), bf16[16,64,256]{2,1,0:T(8,128)(2,1)S(1)}, u32[]{:S(2)}, u32[]{:S(2)}) async-start(bf16[16,64,256]{2,1,0:T(8,128)(2,1)} %bitcast.10), calls=%async_computation.1 | async-start | bytes 1048576 | tf_op jit(solution)/shard_map/all_to_all | solution.py:505
  135.4 12.2 %collective-permute-start.15 = (bf16[64,2048]{1,0:T(8,128)(2,1)}, bf16[64,2048]{1,0:T(8,128)(2,1)S(1)}, u32[]{:S(2)}, u32[]{:S(2)}) collective-permute-start(bf16[64,2048]{1,0:T(8,128)(2,1)} %get-tuple-element.78), channel_id=1, source_target_pairs={{0,4},{4,8},{8,12},{12,0},{16,20},{20,24},{24,28},{28,16},{32,36},... | collective-permute-start | bytes 786440 | tf_op jit(solution)/shard_map/ppermute | solution.py:34
  135.4 13.1 %collective-permute-start.16 = (bf16[64,2048]{1,0:T(8,128)(2,1)}, bf16[64,2048]{1,0:T(8,128)(2,1)S(1)}, u32[]{:S(2)}, u32[]{:S(2)}) collective-permute-start(bf16[64,2048]{1,0:T(8,128)(2,1)} %get-tuple-element.79), channel_id=1, source_target_pairs={{0,12},{4,0},{8,4},{12,8},{16,28},{20,16},{24,20},{28,24},{32,44},... | collective-permute-start | bytes 786440 | tf_op jit(solution)/shard_map/ppermute | solution.py:34
  138.6 9.9 %collective-permute-start.17 = (bf16[64,2048]{1,0:T(8,128)(2,1)}, bf16[64,2048]{1,0:T(8,128)(2,1)S(1)}, u32[]{:S(2)}, u32[]{:S(2)}) collective-permute-start(bf16[64,2048]{1,0:T(8,128)(2,1)} %get-tuple-element.80), channel_id=1, source_target_pairs={{0,8},{4,12},{8,0},{12,4},{16,24},{20,28},{24,16},{28,20},{32,40},... | collective-permute-start | bytes 786440 | tf_op jit(solution)/shard_map/ppermute | solution.py:34
  139.3 1.0 copy-start.17
  144.3 7.9 %collective-permute-start.21 = (bf16[64,2048]{1,0:T(8,128)(2,1)}, bf16[64,2048]{1,0:T(8,128)(2,1)S(1)}, u32[]{:S(2)}, u32[]{:S(2)}) collective-permute-start(bf16[64,2048]{1,0:T(8,128)(2,1)} %get-tuple-element.93), channel_id=1, source_target_pairs={{0,16},{4,20},{8,24},{12,28},{16,32},{20,36},{24,40},{28,44},{32,4... | collective-permute-start | bytes 786440 | tf_op jit(solution)/shard_map/ppermute | solution.py:34
  144.6 10.0 %collective-permute-start.22 = (bf16[64,2048]{1,0:T(8,128)(2,1)}, bf16[64,2048]{1,0:T(8,128)(2,1)S(1)}, u32[]{:S(2)}, u32[]{:S(2)}) collective-permute-start(bf16[64,2048]{1,0:T(8,128)(2,1)} %get-tuple-element.94), channel_id=1, source_target_pairs={{0,48},{4,52},{8,56},{12,60},{16,0},{20,4},{24,8},{28,12},{32,16},... | collective-permute-start | bytes 786440 | tf_op jit(solution)/shard_map/ppermute | solution.py:34
  147.6 8.1 %collective-permute-start.23 = (bf16[64,2048]{1,0:T(8,128)(2,1)}, bf16[64,2048]{1,0:T(8,128)(2,1)S(1)}, u32[]{:S(2)}, u32[]{:S(2)}) collective-permute-start(bf16[64,2048]{1,0:T(8,128)(2,1)} %get-tuple-element.95), channel_id=1, source_target_pairs={{0,32},{4,36},{8,40},{12,44},{16,48},{20,52},{24,56},{28,60},{32,0... | collective-permute-start | bytes 786440 | tf_op jit(solution)/shard_map/ppermute | solution.py:34
  155.7 1.0 copy-start.2
  156.6 0.9 copy-start.3
